TPU v7x, 512 devices: a whole 4x8x8 slice. The times are simulated.
512 devices in a mesh: dp: 64 (over y, x, core), mp: 8 (over z).
Axes of the slice: x: 4, y: 8, z: 8, core: 2. Of those that a mesh axis runs over, the one named last changes fastest.
Arguments:
- x_input: bfloat16 [64, 1536, 2048], P('dp', None, 'mp'), may hold values from -24 to 24
- dy_grad: bfloat16 [64, 1536, 2048], P('dp', 'mp'), may hold values from -0.15625 to 0.15625
- error_in: bfloat16 [64, 2048, 2048], P('dp', 'mp'), may hold values from -6 to 6
- q_init: float32 [2048, 64], replicated, may hold values from -0.125 to 0.125
Outputs:
- p_panel: float32 [2048, 64], P('mp')
- q_panel: float32 [2048, 64], replicated
- error_out: bfloat16 [64, 2048, 2048], P('dp', 'mp')
All inputs are finite; a program needn't handle non-finite values.
Results may differ from a plain program's by a relative error of at most 0.0011.
Values may be sent and summed in bfloat16 or wider, within the bound.
A program may use at most 64 MiB of HBM per device.

v0:
```python
import jax
import jax.numpy as jnp
from jax import lax
from jax.sharding import PartitionSpec as P


def orthonormal(panel_rows, gram_matrix):
    factor = jnp.linalg.cholesky(gram_matrix)
    return jax.scipy.linalg.solve_triangular(factor, panel_rows.T, lower=True).T


def local(x_input, dy_grad, error_in, q_init):
    highest = lax.Precision.HIGHEST
    features = x_input[0]
    grad_block = lax.dot_general(
        features,
        lax.all_gather(dy_grad, "mp", axis=1, tiled=True)[0],
        (((0,), (0,)), ((), ())),
        preferred_element_type=jnp.float32,
    )
    corrected = grad_block + error_in[0].astype(jnp.float32)
    p_local = jnp.dot(corrected, q_init, precision=highest)
    p_sum = lax.psum(p_local, "dp")
    gram_matrix = lax.psum(jnp.dot(p_sum.T, p_sum, precision=highest), "mp")
    p_panel = orthonormal(p_sum, gram_matrix)
    q_local = lax.dot_general(corrected, p_panel, (((0,), (0,)), ((), ())), precision=highest)
    q_panel = lax.psum(q_local, ("dp", "mp"))
    approx = jnp.dot(p_panel, q_panel.T, precision=highest)
    error_out = (corrected - approx).astype(jnp.bfloat16)[None]
    return (p_panel, q_panel, error_out)


def solution(mesh):
    in_specs = (P("dp", None, "mp"), P("dp", "mp", None), P("dp", "mp", None), P())
    out_specs = (P("mp", None), P(), P("dp", "mp", None))
    return jax.shard_map(local, mesh=mesh, in_specs=in_specs, out_specs=out_specs, check_vma=False)
```

profile of v0, /device:TPU:1, one launch (start us, length us, event | category | flops | bytes accessed | tf_op | source)
XLA Modules:
  0.0 601.4 jit_solution(15850860745349187699)
XLA Ops:
  7.2 0.0 copy-start
  7.2 0.0 all-gather.2.cloned.1.call-start
  7.2 0.7 all-gather.2.cloned.1.call-update
  7.9 0.0 copy-start.3
  7.9 0.0 all-reduce.3.cloned.1.call-start
  8.0 85.6 %all-gather.2.cloned.1.call-done = bf16[1,1536,2048]{2,1,0:T(8,128)(2,1)} async-done(((bf16[1,192,2048]{2,1,0:T(8,128)(2,1)}), bf16[1,1536,2048]{2,1,0:T(8,128)(2,1)}) %all-gather.2.cloned.1.call-update) | async-done | bytes 6291472 | tf_op jit(solution)/shard_map/all_gather | solution.py:17
  93.5 0.0 copy-done
  93.5 4.8 fusion.2
  98.4 0.0 copy-done.3
  98.4 2.7 fusion.12
  101.1 0.0 all-reduce.3.cloned.1.call-update
  101.1 0.0 all-reduce.5.cloned.1.call-start
  101.1 177.4 %all-reduce.3.cloned.1.call-done = f32[256,64]{0,1:T(8,128)} async-done(((f32[256,64]{0,1:T(8,128)}), f32[256,64]{0,1:T(8,128)}) %all-reduce.3.cloned.1.call-update) | async-done | bytes 65552 | tf_op jit(solution)/shard_map/psum | solution.py:23
  278.6 1.1 fusion.13
  279.7 23.8 %psum.22 = f32[64,64]{0,1:T(8,128)S(1)} all-reduce(f32[64,64]{0,1:T(8,128)S(1)} %fusion.13), channel_id=1, replica_groups=mesh['dp'=64,'mp'=8] {'mp'}, use_global_device_ids=true, to_apply=%region_1.0 | all-reduce | flops 4096 | bytes 32768 | tf_op jit(solution)/shard_map/psum | solution.py:24
  303.5 0.1 copy.8
  303.6 5.8 cholesky.16
  309.5 0.6 compare_reduce_fusion
  310.2 0.7 fusion.8
  310.8 4.9 custom-call.7
  315.7 1.1 fusion.9
  316.8 0.0 copy-start.2
  316.8 2.3 fusion.14
  319.1 0.0 all-reduce.5.cloned.1.call-update
  319.1 271.0 %all-reduce.5.cloned.1.call-done = f32[2048,64]{0,1:T(8,128)} async-done(((f32[2048,64]{0,1:T(8,128)}), f32[2048,64]{0,1:T(8,128)}) %all-reduce.5.cloned.1.call-update) | async-done | bytes 524304 | tf_op jit(solution)/shard_map/psum | solution.py:27
  590.1 0.0 copy-start.1
  590.1 3.9 fusion.6
  594.0 0.0 copy-done.2
  594.0 0.0 copy-done.1
  594.0 0.8 copy.12
  (2 shorter events, 0.0 us)
Async XLA Ops:
  7.2 86.4 %copy-start = (bf16[1,1536,256]{2,1,0:T(8,128)(2,1)S(1)}, bf16[1,1536,256]{2,1,0:T(8,128)(2,1)}, u32[]{:S(2)}) copy-start(bf16[1,1536,256]{2,1,0:T(8,128)(2,1)} %param.4) | copy-start | bytes 2359300
  7.2 86.4 %all-gather.2.cloned.1.call-start = ((), (), s32[]{:S(2)}) async-start(), calls=%async_computation | async-start | bytes 7077888 | tf_op jit(solution)/shard_map/all_gather | solution.py:17
  7.9 90.5 %copy-start.3 = (f32[2048,64]{0,1:T(8,128)S(1)}, f32[2048,64]{0,1:T(8,128)}, u32[]{:S(2)}) copy-start(f32[2048,64]{0,1:T(8,128)} %param.7) | copy-start | bytes 1572868
  7.9 270.6 %all-reduce.3.cloned.1.call-start = ((), (), s32[]{:S(2)}) async-start(), calls=%async_computation.1 | async-start | bytes 131072 | tf_op jit(solution)/shard_map/psum | solution.py:23
  101.1 489.0 %all-reduce.5.cloned.1.call-start = ((), (), s32[]{:S(2)}) async-start(), calls=%async_computation.2 | async-start | bytes 1048576 | tf_op jit(solution)/shard_map/psum | solution.py:27
  316.8 277.2 %copy-start.2 = (f32[64,256]{1,0:T(8,128)}, f32[64,256]{1,0:T(8,128)S(1)}, u32[]{:S(2)}) copy-start(f32[64,256]{1,0:T(8,128)S(1)} %fusion.9) | copy-start | bytes 196612
  590.1 4.0 copy-start.1
Sparse Core Ops, SparseCore 0:
  10.1 83.3 all-gather.1
  101.2 177.3 all-reduce.2
  319.3 270.7 all-reduce.4
where the time goes:
time: 602 us; the launch traced here: 601 us
  waiting for transfers between devices  535 us (89%)
  blocking collectives  23.8 us (4%)
  matrix products  16 us (3%)
  between operations  13.8 us (2%)
  other arithmetic  12.1 us (2%)
    psum x1, waiting for transfers between devices, local(): q_panel = lax.psum(q_local, ('dp', 'mp'))  271 us
    psum x1, waiting for transfers between devices, local(): p_sum = lax.psum(p_local, 'dp')  177 us
    all_gather x1, waiting for transfers between devices, local(): lax.all_gather(dy_grad, 'mp', axis=1, tiled=True)[0]  85.6 us
    psum x1, blocking collectives, local(): gram_matrix = lax.psum(jnp.dot(p_sum.T, p_sum, precision=highest), 'mp')  23.8 us
  transfers between devices with their start and end apart: 3, of which 3 were waited for; matrix products, arithmetic and copies ran while one was open for 0% of the time, Pallas kernels for 0%

commit v1 on v0

v1 whole, which is shorter than its diff:
```python
import jax
import jax.numpy as jnp
from jax import lax
from jax.experimental import pallas as pl
from jax.experimental.pallas import tpu as pltpu
from jax.sharding import PartitionSpec as P

F32, BF16 = jnp.float32, jnp.bfloat16
HIGHEST = lax.Precision.HIGHEST
NZ, NY, NX = 8, 8, 4
NJ = 2 * NX
TOK, FEAT, DOUT, RANK = 192, 256, 2048, 64
CHUNKS = 4
PIECE = TOK // CHUNKS
TILE = 512
N_SEMS = 128

NN = (((1,), (0,)), ((), ()))
NT = (((1,), (1,)), ((), ()))
TN = (((0,), (0,)), ((), ()))


def mm(a, b, dims, precision=None):
    return lax.dot_general(a, b, dims, precision=precision, preferred_element_type=F32)


def split_rows(v):
    high = v.astype(BF16)
    low = (v - high.astype(F32)).astype(BF16)
    return high, low


def split_lanes(v):
    both = v + pltpu.roll(v, RANK, axis=1)
    high = both.astype(BF16).astype(F32)
    lane = lax.broadcasted_iota(jnp.int32, both.shape, 1)
    return jnp.where(lane < RANK, high, both - high).astype(BF16)


def inverse_factor(gram2):
    lane = lax.broadcasted_iota(jnp.int32, gram2.shape, 1)
    row = lax.broadcasted_iota(jnp.int32, gram2.shape, 0)
    rows = lax.broadcasted_iota(jnp.int32, (RANK, 1), 0)
    a = jnp.where(lane < RANK, gram2, jnp.where(lane - RANK == row, 1.0, 0.0))
    for k in range(RANK - 1):
        pivot_row = a[k : k + 1, :]
        scaled = pivot_row * (1.0 / a[k : k + 1, k : k + 1])
        below = jnp.where(rows > k, a[:, k : k + 1], 0.0)
        a = a - below * scaled
    diagonal = jnp.sum(jnp.where(lane == row, a, 0.0), axis=1, keepdims=True)
    root = lax.rsqrt(diagonal)
    root = root * (1.5 - 0.5 * (diagonal * root) * root)
    return jnp.where(lane < RANK, 0.0, a * root)


def kernel(
    x_ref, dy_ref, e_ref, q_ref, p_out, q_out, err_out,
    dyg, xv, ev, qv, yq, acc, part_p, in_pj, in_py, all_p, in_g, all_g, part_x, in_x,
    q_part, in_qc, q_core, in_qx, q_y, in_qy, in_qz, all_qy, all_q, p_keep, err_v,
    send_sem, recv_sem, load_sem,
):
    dp, z = lax.axis_index("dp"), lax.axis_index("mp")
    y, j = lax.div(dp, NJ), lax.rem(dp, NJ)
    x, core = lax.div(j, 2), lax.rem(j, 2)
    counter = iter(range(N_SEMS))
    unsent = []

    at_z = lambda k: (dp, lax.rem(z + k + NZ, NZ))
    at_y = lambda k: (lax.rem(y + k, NY) * NJ + j, z)
    at_j = lambda k: (y * NJ + lax.rem(j + k, NJ), z)
    at_x = lambda k: (y * NJ + lax.rem(x + k, NX) * 2 + core, z)
    at_core = (y * NJ + x * 2 + 1 - core, z)

    def send(src, dst, device):
        n = next(counter)
        copy = pltpu.make_async_remote_copy(
            src_ref=src, dst_ref=dst, send_sem=send_sem.at[n], recv_sem=recv_sem.at[n],
            device_id=device, device_id_type=pl.DeviceIdType.MESH,
        )
        copy.start()
        unsent.append(copy)
        return copy

    loads = [
        pltpu.make_async_copy(src, dst, load_sem.at[n])
        for n, (src, dst) in enumerate(((dy_ref, dyg.at[z]), (q_ref, qv), (x_ref, xv), (e_ref, ev)))
    ]
    for load in loads:
        load.start()

    barrier = pltpu.get_barrier_semaphore()
    peers = [at_z(k) for k in range(1, NZ)] + [at_y(k) for k in range(1, NY)] + [at_j(k) for k in range(1, NJ)]
    for peer in peers:
        pl.semaphore_signal(barrier, inc=1, device_id=peer, device_id_type=pl.DeviceIdType.MESH)

    loads[0].wait()
    loads[1].wait()
    q_halves = jnp.concatenate(split_rows(qv[...]), axis=0)
    yq[z] = split_lanes(mm(dyg[z], q_halves, NT))
    pl.semaphore_wait(barrier, len(peers))

    flows = {
        1: [(h, c) for h in (1, 2, 3) for c in range(CHUNKS)] + [(4, 0), (4, 1)],
        -1: [(h, c) for h in (1, 2, 3) for c in range(CHUNKS)] + [(4, 2), (4, 3)],
    }
    bulk = {}

    def bulk_send(way, hop, c):
        block = lax.rem(z - way * (hop - 1) + NZ, NZ)
        ref = dyg.at[block, pl.ds(c * PIECE, PIECE)]
        bulk[way, hop, c] = send(ref, ref, at_z(way))

    def bulk_forward(n):
        for way in (1, -1):
            hop, c = flows[way][n]
            bulk[way, hop, c].wait_recv()
            if (hop + 1, c) in flows[way]:
                bulk_send(way, hop + 1, c)

    def add_grad(block):
        @pl.loop(0, DOUT // TILE)
        def _(t):
            cols = pl.ds(pl.multiple_of(t * TILE, TILE), TILE)
            acc[:, cols] += mm(xv[block], dyg[block, :, cols], TN)

    right = send(yq.at[z], yq.at[z], at_z(1))
    left = send(yq.at[z], yq.at[z], at_z(-1))
    for c in (0, 1):
        bulk_send(1, 1, c)
        bulk_send(-1, 1, c)
    loads[2].wait()
    loads[3].wait()
    total = mm(q_halves, ev[...], NT) + mm(yq[z], xv[z], TN)
    for hop in (1, 2, 3, 4):
        from_left, from_right = lax.rem(z - hop + NZ, NZ), lax.rem(z + hop, NZ)
        right.wait_recv()
        if hop < 4:
            right = send(yq.at[from_left], yq.at[from_left], at_z(1))
            left.wait_recv()
            if hop < 3:
                left = send(yq.at[from_right], yq.at[from_right], at_z(-1))
            total += mm(yq[from_right], xv[from_right], TN)
        total += mm(yq[from_left], xv[from_left], TN)
    for c in (2, 3):
        bulk_send(1, 1, c)
        bulk_send(-1, 1, c)
    total = total[:RANK] + total[RANK:]

    for k in range(NJ):
        part_p[k] = total[k * 8 : k * 8 + 8]
    copies = [send(part_p.at[lax.rem(j + k, NJ)], in_pj.at[j], at_j(k)) for k in range(1, NJ)]
    in_pj[j] = part_p[j]

    @pl.loop(0, DOUT // TILE)
    def _(t):
        cols = pl.ds(pl.multiple_of(t * TILE, TILE), TILE)
        acc[:, cols] = ev[:, cols].astype(F32) + mm(xv[z], dyg[z, :, cols], TN)

    for copy in copies:
        copy.wait_recv()
    in_py[y] = sum(in_pj[k] for k in range(1, NJ)) + in_pj[0]
    copies = [send(in_py.at[y], in_py.at[y], at_y(k)) for k in range(1, NY)]
    bulk_forward(0)
    for copy in copies:
        copy.wait_recv()
    all_p[j] = sum(in_py[k] for k in range(1, NY)) + in_py[0]
    copies = [send(all_p.at[j], all_p.at[j], at_j(k)) for k in range(1, NJ)]
    for copy in copies:
        copy.wait_recv()
    p_sum = all_p[...].reshape(RANK, FEAT)
    p_twice = jnp.concatenate([p_sum, p_sum], axis=0)

    in_g[z] = mm(all_p[j], p_twice, NT, HIGHEST)
    copies = [send(in_g.at[z], in_g.at[z], at_z(k)) for k in range(1, NZ)]
    bulk_forward(1)
    for copy in copies:
        copy.wait_recv()
    all_g[j] = sum(in_g[k] for k in range(1, NZ)) + in_g[0]
    copies = [send(all_g.at[j], all_g.at[j], at_j(k)) for k in range(1, NJ)]
    bulk_forward(2)
    for copy in copies:
        copy.wait_recv()
    inverse = inverse_factor(all_g[...].reshape(RANK, 2 * RANK))
    p_t = mm(inverse, p_twice, NN, HIGHEST)
    p_keep[...] = p_t
    p_store = pltpu.make_async_copy(p_keep, p_out, load_sem.at[4])
    p_store.start()
    p_high, p_low = split_rows(p_t)
    p_halves = jnp.concatenate([p_high, p_low], axis=0)

    copies = []
    for k in (4, 3, 5, 2, 6, 1, 7):
        block = lax.rem(z + k, NZ)
        part_x[block] = split_lanes(mm(xv[block], p_halves, NT))
        copies.append(send(part_x.at[block], in_x.at[z], at_z(k)))
    in_x[z] = split_lanes(mm(xv[z], p_halves, NT))
    bulk_forward(3)
    add_grad(lax.rem(z + NZ - 1, NZ))
    add_grad(lax.rem(z + 1, NZ))
    bulk_forward(4)
    for copy in copies:
        copy.wait_recv()
    xp = split_lanes(sum(in_x[k].astype(F32) for k in range(1, NZ)) + in_x[0].astype(F32))
    bulk_forward(5)

    for t in range(DOUT // TILE):
        cols = slice(t * TILE, t * TILE + TILE)
        tile = mm(xp, dyg[z, :, cols], TN) + mm(p_halves, ev[:, cols], NN)
        tile = tile[:RANK] + tile[RANK:]
        for k in range(8):
            q_part[k // 4, k % 4, :, cols] = tile[k * 8 : k * 8 + 8]
    copy = send(q_part.at[1 - core], in_qc, at_core)
    bulk_forward(6)
    copy.wait_recv()
    for k in range(NX):
        q_core[k] = q_part[core, k] + in_qc[k]
    copies = [send(q_core.at[lax.rem(x + k, NX)], in_qx.at[x], at_x(k)) for k in range(1, NX)]
    in_qx[x] = q_core[x]
    bulk_forward(7)
    for copy in copies:
        copy.wait_recv()
    rows = (in_qx[0] + in_qx[1]) + (in_qx[2] + in_qx[3])
    for k in range(NY):
        q_y[k] = rows[:, k * 256 : k * 256 + 256]
    copies = [send(q_y.at[lax.rem(y + k, NY)], in_qy.at[y], at_y(k)) for k in range(1, NY)]
    in_qy[y] = q_y[y]
    for copy in copies:
        copy.wait_recv()
    in_qz[z] = sum(in_qy[k] for k in range(1, NY)) + in_qy[0]
    copies = [send(in_qz.at[z], in_qz.at[z], at_z(k)) for k in range(1, NZ)]
    add_grad(lax.rem(z + NZ - 2, NZ))
    add_grad(lax.rem(z + 2, NZ))
    bulk_forward(8)
    for copy in copies:
        copy.wait_recv()
    all_qy[y] = sum(in_qz[k] for k in range(1, NZ)) + in_qz[0]
    copies = [send(all_qy.at[y], all_qy.at[y], at_y(k)) for k in range(1, NY)]
    bulk_forward(9)
    for copy in copies:
        copy.wait_recv()
    mine = core * NX + x
    for k in range(NY):
        all_q[mine, :, k * 256 : k * 256 + 256] = all_qy[k]
    copies = [send(all_q.at[mine], all_q.at[mine], at_x(k)) for k in range(1, NX)]
    across = [send(all_q.at[mine], all_q.at[mine], at_core)]
    for k, copy in enumerate(copies):
        copy.wait_recv()
        slot = core * NX + lax.rem(x - (k + 1) + NX, NX)
        across.append(send(all_q.at[slot], all_q.at[slot], at_core))
    bulk_forward(10)
    bulk_forward(11)
    for copy in across:
        copy.wait_recv()
    q_store = pltpu.make_async_copy(all_q, q_out, load_sem.at[5])
    q_store.start()
    p_cat = jnp.concatenate([p_high, p_high, p_low], axis=0)

    @pl.loop(0, DOUT // TILE)
    def _(t):
        cols = pl.ds(pl.multiple_of(t * TILE, TILE), TILE)
        q_high, q_low = split_rows(all_q[:, :, cols].reshape(RANK, TILE))
        acc[:, cols] -= mm(p_cat, jnp.concatenate([q_high, q_low, q_high], axis=0), TN)

    add_grad(lax.rem(z + NZ - 3, NZ))
    add_grad(lax.rem(z + 3, NZ))
    bulk_forward(12)
    bulk_forward(13)
    far = lax.rem(z + 4, NZ)
    stores = []
    for t in range(DOUT // TILE):
        cols = slice(t * TILE, t * TILE + TILE)
        err_v[:, cols] = (acc[:, cols] + mm(xv[far], dyg[far, :, cols], TN)).astype(BF16)
        store = pltpu.make_async_copy(err_v.at[:, cols], err_out.at[:, cols], load_sem.at[6 + t])
        store.start()
        stores.append(store)
    for copy in unsent:
        copy.wait_send()
    p_store.wait()
    q_store.wait()
    for store in stores:
        store.wait()


def local(x_input, dy_grad, error_in, q_init):
    anywhere = pl.BlockSpec(memory_space=pl.ANY)
    vmem = lambda *shape, dtype=F32: pltpu.VMEM(shape, dtype)
    p_t, q_t, err = pl.pallas_call(
        kernel,
        out_shape=(
            jax.ShapeDtypeStruct((RANK, FEAT), F32),
            jax.ShapeDtypeStruct((8, 8, DOUT), F32),
            jax.ShapeDtypeStruct((FEAT, DOUT), BF16),
        ),
        in_specs=[anywhere] * 4,
        out_specs=(anywhere,) * 3,
        scratch_shapes=[
            vmem(NZ, TOK, DOUT, dtype=BF16),
            vmem(NZ, TOK, FEAT, dtype=BF16),
            vmem(FEAT, DOUT, dtype=BF16),
            vmem(RANK, DOUT),
            vmem(NZ, TOK, 2 * RANK, dtype=BF16),
            vmem(FEAT, DOUT),
            vmem(NJ, 8, FEAT), vmem(NJ, 8, FEAT), vmem(NY, 8, FEAT), vmem(NJ, 8, FEAT),
            vmem(NZ, 8, 2 * RANK), vmem(NJ, 8, 2 * RANK),
            vmem(NZ, TOK, 2 * RANK, dtype=BF16), vmem(NZ, TOK, 2 * RANK, dtype=BF16),
            vmem(2, NX, 8, DOUT), vmem(NX, 8, DOUT), vmem(NX, 8, DOUT), vmem(NX, 8, DOUT),
            vmem(NY, 8, FEAT), vmem(NY, 8, FEAT), vmem(NZ, 8, FEAT), vmem(NY, 8, FEAT),
            vmem(8, 8, DOUT),
            vmem(RANK, FEAT),
            vmem(FEAT, DOUT, dtype=BF16),
            pltpu.SemaphoreType.DMA((N_SEMS,)),
            pltpu.SemaphoreType.DMA((N_SEMS,)),
            pltpu.SemaphoreType.DMA((10,)),
        ],
        compiler_params=pltpu.CompilerParams(
            collective_id=0, has_side_effects=True, vmem_limit_bytes=48 * 1024 * 1024
        ),
        cost_estimate=pl.CostEstimate(flops=2 * 10**9, bytes_accessed=6 * 10**6, transcendentals=0),
    )(x_input.reshape(NZ, TOK, FEAT), dy_grad[0], error_in[0], q_init.T)
    return p_t.T, q_t.reshape(RANK, DOUT).T, err[None]


def solution(mesh):
    in_specs = (P("dp", None, "mp"), P("dp", "mp", None), P("dp", "mp", None), P())
    out_specs = (P("mp", None), P(), P("dp", "mp", None))
    return jax.shard_map(local, mesh=mesh, in_specs=in_specs, out_specs=out_specs, check_vma=False)
```

time: 602 us -> 124 us (0.21)
  waiting for transfers between devices: 535 us -> 0 us
  Pallas kernels: 0 us -> 115 us
  blocking collectives: 23.8 us -> 0 us
  matrix products: 16 us -> 0 us
  between operations: 13.8 us -> 0.65 us
  other arithmetic: 12.1 us -> 0 us
  local copies, waits for them, and re-layouts: 0.89 us -> 6.92 us
    psum x2 -> x0, waiting for transfers between devices: 448 us -> none  [the longest x1 271 us: local(): q_panel = lax.psum(q_local, ('dp', 'mp'))]
    pallas_call x0 -> x1, Pallas kernels: none -> 115 us  [local(): pl.pallas_call(kernel, out_shape=(jax.ShapeDtypeStruct((RANK, FEAT), F32)...]
    all_gather x1 -> x0, waiting for transfers between devices: 85.6 us -> none  [local(): lax.all_gather(dy_grad, 'mp', axis=1, tiled=True)[0]]
    psum x1 -> x0, blocking collectives: 23.8 us -> none  [local(): gram_matrix = lax.psum(jnp.dot(p_sum.T, p_sum, precision=highest), 'mp')]
    dot_general x5 -> x0, matrix products: 14.8 us -> none  [the longest x1 4.85 us: local(): lax.dot_general(features, lax.all_gather(dy_grad, 'mp', axis=1, tiled=Tru...]
    another operation x5 -> x0, other arithmetic: 12.1 us -> none  [the longest x3 6.52 us: orthonormal(): factor = jnp.linalg.cholesky(gram_matrix)]
    unnamed x9 -> x11, local copies, waits for them, and re-layouts: 0.82 us -> 6.92 us
  transfers between devices with their start and end apart: 3 -> 0, of which waited for: 3 -> 0; matrix products, arithmetic and copies ran while one was open for 0% -> 0% of each run, Pallas kernels for 0% -> 0%
where the time goes in v1:
time: 124 us; the launch traced here: 122 us
  Pallas kernels  115 us (93%)
  local copies, waits for them, and re-layouts  6.92 us (6%)
    pallas_call x1, Pallas kernels, local(): pl.pallas_call(kernel, out_shape=(jax.ShapeDtypeStruct((RANK, FEAT), F32)...  115 us
    unnamed x11, local copies, waits for them, and re-layouts  6.92 us

profile of v1, /device:TPU:1, one launch (start us, length us, event | category | flops | bytes accessed | tf_op | source)
XLA Modules:
  0.0 122.4 jit_solution(5474035582871842734)
XLA Ops:
  0.6 0.0 copy-start
  0.6 1.2 copy-done
  1.9 0.0 copy-start.1
  1.9 1.1 copy-done.1
  3.0 0.0 copy-start.2
  3.0 1.1 copy-done.2
  4.1 0.0 copy-start.3
  4.1 1.0 copy-done.3
  5.2 114.9 %shard_map.67 = (f32[64,256]{1,0:T(8,128)S(1)}, f32[8,8,2048]{2,1,0:T(8,128)S(1)}, bf16[256,2048]{1,0:T(8,128)(2,1)S(1)}) custom-call(bf16[8,192,256]{2,1,0:T(8,128)(2,1)S(1)} %bitcast.13, bf16[192,2048]{1,0:T(8,128)(2,1)S(1)} %bitcast.14, bf16[256,2048]{1,0:T(8,128)(2,1)S(1)} %bitcast.12, f32[64,2048]{1,0:T(8,128)S(1)} %bitcast.15), custom_call_target="tpu_custom_call" | custom-call | flops 2000000000 | bytes 6000000 | tf_op jit(solution)/shard_map/pallas_call | solution.py:287
  120.0 0.6 copy.10
  120.7 0.8 copy.11
  121.5 1.0 copy.12
Async XLA Ops:
  0.6 1.2 %copy-start = (bf16[1,256,2048]{2,1,0:T(8,128)(2,1)S(1)}, bf16[1,256,2048]{2,1,0:T(8,128)(2,1)}, u32[]{:S(2)}) copy-start(bf16[1,256,2048]{2,1,0:T(8,128)(2,1)} %param.6) | copy-start | bytes 3145732
  1.9 1.1 copy-start.1
  3.0 1.1 copy-start.2
  4.1 1.0 copy-start.3

commit v2 on v1

--- a/solution.py
+++ b/solution.py
@@ -14,6 +14,7 @@
 PIECE = TOK // CHUNKS
 TILE = 512
 N_SEMS = 128
+NEAR = 2
 
 NN = (((1,), (0,)), ((), ()))
 NT = (((1,), (1,)), ((), ()))
@@ -37,7 +38,7 @@
     return jnp.where(lane < RANK, high, both - high).astype(BF16)
 
 
-def inverse_factor(gram2):
+def inverse_factor(gram2, between):
     lane = lax.broadcasted_iota(jnp.int32, gram2.shape, 1)
     row = lax.broadcasted_iota(jnp.int32, gram2.shape, 0)
     rows = lax.broadcasted_iota(jnp.int32, (RANK, 1), 0)
@@ -47,6 +48,7 @@
         scaled = pivot_row * (1.0 / a[k : k + 1, k : k + 1])
         below = jnp.where(rows > k, a[:, k : k + 1], 0.0)
         a = a - below * scaled
+        between(k)
     diagonal = jnp.sum(jnp.where(lane == row, a, 0.0), axis=1, keepdims=True)
     root = lax.rsqrt(diagonal)
     root = root * (1.5 - 0.5 * (diagonal * root) * root)
@@ -123,27 +125,17 @@
             cols = pl.ds(pl.multiple_of(t * TILE, TILE), TILE)
             acc[:, cols] += mm(xv[block], dyg[block, :, cols], TN)
 
-    right = send(yq.at[z], yq.at[z], at_z(1))
-    left = send(yq.at[z], yq.at[z], at_z(-1))
-    for c in (0, 1):
+    copies = [send(yq.at[z], yq.at[z], at_z(k)) for k in (4, 3, 5, 2, 6, 1, 7)]
+    for c in range(CHUNKS):
         bulk_send(1, 1, c)
         bulk_send(-1, 1, c)
     loads[2].wait()
     loads[3].wait()
     total = mm(q_halves, ev[...], NT) + mm(yq[z], xv[z], TN)
-    for hop in (1, 2, 3, 4):
-        from_left, from_right = lax.rem(z - hop + NZ, NZ), lax.rem(z + hop, NZ)
-        right.wait_recv()
-        if hop < 4:
-            right = send(yq.at[from_left], yq.at[from_left], at_z(1))
-            left.wait_recv()
-            if hop < 3:
-                left = send(yq.at[from_right], yq.at[from_right], at_z(-1))
-            total += mm(yq[from_right], xv[from_right], TN)
-        total += mm(yq[from_left], xv[from_left], TN)
-    for c in (2, 3):
-        bulk_send(1, 1, c)
-        bulk_send(-1, 1, c)
+    for k, copy in reversed(list(zip((4, 3, 5, 2, 6, 1, 7), copies))):
+        copy.wait_recv()
+        block = lax.rem(z - k + NZ, NZ)
+        total += mm(yq[block], xv[block], TN)
     total = total[:RANK] + total[RANK:]
 
     for k in range(NJ):
@@ -156,15 +148,17 @@
         cols = pl.ds(pl.multiple_of(t * TILE, TILE), TILE)
         acc[:, cols] = ev[:, cols].astype(F32) + mm(xv[z], dyg[z, :, cols], TN)
 
+    bulk_forward(0)
     for copy in copies:
         copy.wait_recv()
     in_py[y] = sum(in_pj[k] for k in range(1, NJ)) + in_pj[0]
     copies = [send(in_py.at[y], in_py.at[y], at_y(k)) for k in range(1, NY)]
-    bulk_forward(0)
+    bulk_forward(1)
     for copy in copies:
         copy.wait_recv()
     all_p[j] = sum(in_py[k] for k in range(1, NY)) + in_py[0]
     copies = [send(all_p.at[j], all_p.at[j], at_j(k)) for k in range(1, NJ)]
+    bulk_forward(2)
     for copy in copies:
         copy.wait_recv()
     p_sum = all_p[...].reshape(RANK, FEAT)
@@ -172,15 +166,19 @@
 
     in_g[z] = mm(all_p[j], p_twice, NT, HIGHEST)
     copies = [send(in_g.at[z], in_g.at[z], at_z(k)) for k in range(1, NZ)]
-    bulk_forward(1)
+    bulk_forward(3)
+    add_grad(lax.rem(z + NZ - 1, NZ))
+    add_grad(lax.rem(z + 1, NZ))
     for copy in copies:
         copy.wait_recv()
     all_g[j] = sum(in_g[k] for k in range(1, NZ)) + in_g[0]
     copies = [send(all_g.at[j], all_g.at[j], at_j(k)) for k in range(1, NJ)]
-    bulk_forward(2)
-    for copy in copies:
-        copy.wait_recv()
-    inverse = inverse_factor(all_g[...].reshape(RANK, 2 * RANK))
+    bulk_forward(4)
+    for copy in copies:
+        copy.wait_recv()
+    steps = {20: 5, 40: 6}
+    between = lambda k: bulk_forward(steps[k]) if k in steps else None
+    inverse = inverse_factor(all_g[...].reshape(RANK, 2 * RANK), between)
     p_t = mm(inverse, p_twice, NN, HIGHEST)
     p_keep[...] = p_t
     p_store = pltpu.make_async_copy(p_keep, p_out, load_sem.at[4])
@@ -188,35 +186,34 @@
     p_high, p_low = split_rows(p_t)
     p_halves = jnp.concatenate([p_high, p_low], axis=0)
 
+    far_steps = [k for k in (4, 3, 5, 2, 6, 1, 7) if min(k, NZ - k) > NEAR]
     copies = []
-    for k in (4, 3, 5, 2, 6, 1, 7):
+    for k in far_steps:
         block = lax.rem(z + k, NZ)
         part_x[block] = split_lanes(mm(xv[block], p_halves, NT))
         copies.append(send(part_x.at[block], in_x.at[z], at_z(k)))
-    in_x[z] = split_lanes(mm(xv[z], p_halves, NT))
-    bulk_forward(3)
-    add_grad(lax.rem(z + NZ - 1, NZ))
-    add_grad(lax.rem(z + 1, NZ))
-    bulk_forward(4)
-    for copy in copies:
-        copy.wait_recv()
-    xp = split_lanes(sum(in_x[k].astype(F32) for k in range(1, NZ)) + in_x[0].astype(F32))
-    bulk_forward(5)
+    bulk_forward(7)
+    for hop in range(2, NEAR + 1):
+        add_grad(lax.rem(z + NZ - hop, NZ))
+        add_grad(lax.rem(z + hop, NZ))
+    for copy in copies:
+        copy.wait_recv()
+    xp = split_lanes(sum(in_x[lax.rem(z + NZ - k, NZ)].astype(F32) for k in far_steps))
 
     for t in range(DOUT // TILE):
         cols = slice(t * TILE, t * TILE + TILE)
-        tile = mm(xp, dyg[z, :, cols], TN) + mm(p_halves, ev[:, cols], NN)
-        tile = tile[:RANK] + tile[RANK:]
+        near_high, near_low = split_rows(acc[:, cols])
+        tile = mm(xp, dyg[z, :, cols], TN) + mm(p_halves, near_high, NN)
+        tile = tile[:RANK] + tile[RANK:] + mm(p_high, near_low, NN)
         for k in range(8):
             q_part[k // 4, k % 4, :, cols] = tile[k * 8 : k * 8 + 8]
     copy = send(q_part.at[1 - core], in_qc, at_core)
-    bulk_forward(6)
+    bulk_forward(8)
     copy.wait_recv()
     for k in range(NX):
         q_core[k] = q_part[core, k] + in_qc[k]
     copies = [send(q_core.at[lax.rem(x + k, NX)], in_qx.at[x], at_x(k)) for k in range(1, NX)]
     in_qx[x] = q_core[x]
-    bulk_forward(7)
     for copy in copies:
         copy.wait_recv()
     rows = (in_qx[0] + in_qx[1]) + (in_qx[2] + in_qx[3])
@@ -224,18 +221,20 @@
         q_y[k] = rows[:, k * 256 : k * 256 + 256]
     copies = [send(q_y.at[lax.rem(y + k, NY)], in_qy.at[y], at_y(k)) for k in range(1, NY)]
     in_qy[y] = q_y[y]
+    bulk_forward(9)
     for copy in copies:
         copy.wait_recv()
     in_qz[z] = sum(in_qy[k] for k in range(1, NY)) + in_qy[0]
     copies = [send(in_qz.at[z], in_qz.at[z], at_z(k)) for k in range(1, NZ)]
-    add_grad(lax.rem(z + NZ - 2, NZ))
-    add_grad(lax.rem(z + 2, NZ))
-    bulk_forward(8)
+    bulk_forward(10)
+    bulk_forward(11)
     for copy in copies:
         copy.wait_recv()
     all_qy[y] = sum(in_qz[k] for k in range(1, NZ)) + in_qz[0]
     copies = [send(all_qy.at[y], all_qy.at[y], at_y(k)) for k in range(1, NY)]
-    bulk_forward(9)
+    for hop in range(NEAR + 1, 4):
+        add_grad(lax.rem(z + NZ - hop, NZ))
+        add_grad(lax.rem(z + hop, NZ))
     for copy in copies:
         copy.wait_recv()
     mine = core * NX + x
@@ -247,29 +246,20 @@
         copy.wait_recv()
         slot = core * NX + lax.rem(x - (k + 1) + NX, NX)
         across.append(send(all_q.at[slot], all_q.at[slot], at_core))
-    bulk_forward(10)
-    bulk_forward(11)
+    bulk_forward(12)
+    bulk_forward(13)
+    add_grad(lax.rem(z + 4, NZ))
     for copy in across:
         copy.wait_recv()
     q_store = pltpu.make_async_copy(all_q, q_out, load_sem.at[5])
     q_store.start()
     p_cat = jnp.concatenate([p_high, p_high, p_low], axis=0)
-
-    @pl.loop(0, DOUT // TILE)
-    def _(t):
-        cols = pl.ds(pl.multiple_of(t * TILE, TILE), TILE)
-        q_high, q_low = split_rows(all_q[:, :, cols].reshape(RANK, TILE))
-        acc[:, cols] -= mm(p_cat, jnp.concatenate([q_high, q_low, q_high], axis=0), TN)
-
-    add_grad(lax.rem(z + NZ - 3, NZ))
-    add_grad(lax.rem(z + 3, NZ))
-    bulk_forward(12)
-    bulk_forward(13)
-    far = lax.rem(z + 4, NZ)
     stores = []
     for t in range(DOUT // TILE):
         cols = slice(t * TILE, t * TILE + TILE)
-        err_v[:, cols] = (acc[:, cols] + mm(xv[far], dyg[far, :, cols], TN)).astype(BF16)
+        q_high, q_low = split_rows(all_q[:, :, cols].reshape(RANK, TILE))
+        approx = mm(p_cat, jnp.concatenate([q_high, q_low, q_high], axis=0), TN)
+        err_v[:, cols] = (acc[:, cols] - approx).astype(BF16)
         store = pltpu.make_async_copy(err_v.at[:, cols], err_out.at[:, cols], load_sem.at[6 + t])
         store.start()
         stores.append(store)
@@ -313,7 +303,7 @@
             pltpu.SemaphoreType.DMA((10,)),
         ],
         compiler_params=pltpu.CompilerParams(
-            collective_id=0, has_side_effects=True, vmem_limit_bytes=48 * 1024 * 1024
+            collective_id=0, has_side_effects=True, vmem_limit_bytes=60 * 1024 * 1024
         ),
         cost_estimate=pl.CostEstimate(flops=2 * 10**9, bytes_accessed=6 * 10**6, transcendentals=0),
     )(x_input.reshape(NZ, TOK, FEAT), dy_grad[0], error_in[0], q_init.T)

time: 124 us -> 118 us (0.952)
  Pallas kernels: 115 us -> 112 us
  local copies, waits for them, and re-layouts: 6.92 us -> 4.41 us
    unnamed x11 -> x5, local copies, waits for them, and re-layouts: 6.92 us -> 4.41 us
    pallas_call x1, Pallas kernels: 115 us -> 112 us  [local(): pl.pallas_call(kernel, out_shape=(jax.ShapeDtypeStruct((RANK, FEAT), F32)...]
where the time goes in v2:
time: 118 us
  Pallas kernels  112 us (95%)
  local copies, waits for them, and re-layouts  4.41 us (4%)
    pallas_call x1, Pallas kernels, local(): pl.pallas_call(kernel, out_shape=(jax.ShapeDtypeStruct((RANK, FEAT), F32)...  112 us
    unnamed x5, local copies, waits for them, and re-layouts  4.41 us

profile of v2, /device:TPU:1, one launch (start us, length us, event | category | flops | bytes accessed | tf_op | source)
XLA Modules:
  0.0 117.5 jit_solution(8962699469832693240)
XLA Ops:
  0.6 112.5 %shard_map.67 = (f32[64,256]{1,0:T(8,128)}, f32[8,8,2048]{2,1,0:T(8,128)}, bf16[256,2048]{1,0:T(8,128)(2,1)}) custom-call(bf16[8,192,256]{2,1,0:T(8,128)(2,1)} %bitcast.13, bf16[192,2048]{1,0:T(8,128)(2,1)} %bitcast.14, bf16[256,2048]{1,0:T(8,128)(2,1)} %bitcast.12, f32[64,2048]{1,0:T(8,128)} %bitcast.15), custom_call_target="tpu_custom_call" | custom-call | flops 2000000000 | bytes 6000000 | tf_op jit(solution)/shard_map/pallas_call | solution.py:277
  113.1 0.0 copy-start
  113.1 1.6 %copy.10 = f32[256,64]{0,1:T(8,128)} copy(f32[256,64]{0,1:T(8,128)} %bitcast.11) | data formatting | bytes 131072
  114.7 1.9 %copy.11 = f32[2048,64]{0,1:T(8,128)} copy(f32[2048,64]{0,1:T(8,128)} %bitcast.10) | data formatting | bytes 1048576
  116.5 0.0 copy-done
  116.5 1.0 copy.12
Async XLA Ops:
  113.1 3.4 %copy-start = (bf16[256,2048]{1,0:T(8,128)(2,1)S(1)}, bf16[256,2048]{1,0:T(8,128)(2,1)}, u32[]{:S(2)}) copy-start(bf16[256,2048]{1,0:T(8,128)(2,1)} %get-tuple-element.8) | copy-start | bytes 3145732

commit v3 on v2

--- a/solution.py
+++ b/solution.py
@@ -13,6 +13,7 @@
 CHUNKS = 4
 PIECE = TOK // CHUNKS
 TILE = 512
+PIVOTS = 4
 N_SEMS = 128
 NEAR = 2
 
@@ -43,11 +44,16 @@
     row = lax.broadcasted_iota(jnp.int32, gram2.shape, 0)
     rows = lax.broadcasted_iota(jnp.int32, (RANK, 1), 0)
     a = jnp.where(lane < RANK, gram2, jnp.where(lane - RANK == row, 1.0, 0.0))
-    for k in range(RANK - 1):
-        pivot_row = a[k : k + 1, :]
-        scaled = pivot_row * (1.0 / a[k : k + 1, k : k + 1])
-        below = jnp.where(rows > k, a[:, k : k + 1], 0.0)
-        a = a - below * scaled
+    for k in range(0, RANK, PIVOTS):
+        columns = [jnp.broadcast_to(a[:, k + i : k + i + 1], a.shape) for i in range(PIVOTS)]
+        lines = [a[k + i : k + i + 1, :] for i in range(PIVOTS)]
+        for i in range(PIVOTS):
+            here = slice(k + i, k + i + 1)
+            factor = jnp.where(rows > k + i, columns[i] * (1.0 / columns[i][here]), 0.0)
+            for later in range(i + 1, PIVOTS):
+                columns[later] = columns[later] - factor * columns[later][here]
+                lines[later] = lines[later] - factor[k + later : k + later + 1] * lines[i]
+            a = a - factor * lines[i]
         between(k)
     diagonal = jnp.sum(jnp.where(lane == row, a, 0.0), axis=1, keepdims=True)
     root = lax.rsqrt(diagonal)
@@ -83,6 +89,12 @@
         unsent.append(copy)
         return copy
 
+    def receive(copies):
+        while len(unsent) > len(copies):
+            unsent.pop(0).wait_send()
+        for copy in copies:
+            copy.wait_recv()
+
     loads = [
         pltpu.make_async_copy(src, dst, load_sem.at[n])
         for n, (src, dst) in enumerate(((dy_ref, dyg.at[z]), (q_ref, qv), (x_ref, xv), (e_ref, ev)))
@@ -111,6 +123,7 @@
         block = lax.rem(z - way * (hop - 1) + NZ, NZ)
         ref = dyg.at[block, pl.ds(c * PIECE, PIECE)]
         bulk[way, hop, c] = send(ref, ref, at_z(way))
+        unsent.pop()
 
     def bulk_forward(n):
         for way in (1, -1):
@@ -118,6 +131,8 @@
             bulk[way, hop, c].wait_recv()
             if (hop + 1, c) in flows[way]:
                 bulk_send(way, hop + 1, c)
+            if n >= 2:
+                bulk[(way, *flows[way][n - 2])].wait_send()
 
     def add_grad(block):
         @pl.loop(0, DOUT // TILE)
@@ -149,18 +164,15 @@
         acc[:, cols] = ev[:, cols].astype(F32) + mm(xv[z], dyg[z, :, cols], TN)
 
     bulk_forward(0)
-    for copy in copies:
-        copy.wait_recv()
+    receive(copies)
     in_py[y] = sum(in_pj[k] for k in range(1, NJ)) + in_pj[0]
     copies = [send(in_py.at[y], in_py.at[y], at_y(k)) for k in range(1, NY)]
     bulk_forward(1)
-    for copy in copies:
-        copy.wait_recv()
+    receive(copies)
     all_p[j] = sum(in_py[k] for k in range(1, NY)) + in_py[0]
     copies = [send(all_p.at[j], all_p.at[j], at_j(k)) for k in range(1, NJ)]
     bulk_forward(2)
-    for copy in copies:
-        copy.wait_recv()
+    receive(copies)
     p_sum = all_p[...].reshape(RANK, FEAT)
     p_twice = jnp.concatenate([p_sum, p_sum], axis=0)
 
@@ -169,13 +181,11 @@
     bulk_forward(3)
     add_grad(lax.rem(z + NZ - 1, NZ))
     add_grad(lax.rem(z + 1, NZ))
-    for copy in copies:
-        copy.wait_recv()
+    receive(copies)
     all_g[j] = sum(in_g[k] for k in range(1, NZ)) + in_g[0]
     copies = [send(all_g.at[j], all_g.at[j], at_j(k)) for k in range(1, NJ)]
     bulk_forward(4)
-    for copy in copies:
-        copy.wait_recv()
+    receive(copies)
     steps = {20: 5, 40: 6}
     between = lambda k: bulk_forward(steps[k]) if k in steps else None
     inverse = inverse_factor(all_g[...].reshape(RANK, 2 * RANK), between)
@@ -196,8 +206,7 @@
     for hop in range(2, NEAR + 1):
         add_grad(lax.rem(z + NZ - hop, NZ))
         add_grad(lax.rem(z + hop, NZ))
-    for copy in copies:
-        copy.wait_recv()
+    receive(copies)
     xp = split_lanes(sum(in_x[lax.rem(z + NZ - k, NZ)].astype(F32) for k in far_steps))
 
     for t in range(DOUT // TILE):
@@ -209,34 +218,30 @@
             q_part[k // 4, k % 4, :, cols] = tile[k * 8 : k * 8 + 8]
     copy = send(q_part.at[1 - core], in_qc, at_core)
     bulk_forward(8)
-    copy.wait_recv()
+    receive([copy])
     for k in range(NX):
         q_core[k] = q_part[core, k] + in_qc[k]
     copies = [send(q_core.at[lax.rem(x + k, NX)], in_qx.at[x], at_x(k)) for k in range(1, NX)]
     in_qx[x] = q_core[x]
-    for copy in copies:
-        copy.wait_recv()
+    receive(copies)
     rows = (in_qx[0] + in_qx[1]) + (in_qx[2] + in_qx[3])
     for k in range(NY):
         q_y[k] = rows[:, k * 256 : k * 256 + 256]
     copies = [send(q_y.at[lax.rem(y + k, NY)], in_qy.at[y], at_y(k)) for k in range(1, NY)]
     in_qy[y] = q_y[y]
     bulk_forward(9)
-    for copy in copies:
-        copy.wait_recv()
+    receive(copies)
     in_qz[z] = sum(in_qy[k] for k in range(1, NY)) + in_qy[0]
     copies = [send(in_qz.at[z], in_qz.at[z], at_z(k)) for k in range(1, NZ)]
     bulk_forward(10)
     bulk_forward(11)
-    for copy in copies:
-        copy.wait_recv()
+    receive(copies)
     all_qy[y] = sum(in_qz[k] for k in range(1, NZ)) + in_qz[0]
     copies = [send(all_qy.at[y], all_qy.at[y], at_y(k)) for k in range(1, NY)]
     for hop in range(NEAR + 1, 4):
         add_grad(lax.rem(z + NZ - hop, NZ))
         add_grad(lax.rem(z + hop, NZ))
-    for copy in copies:
-        copy.wait_recv()
+    receive(copies)
     mine = core * NX + x
     for k in range(NY):
         all_q[mine, :, k * 256 : k * 256 + 256] = all_qy[k]
@@ -249,8 +254,7 @@
     bulk_forward(12)
     bulk_forward(13)
     add_grad(lax.rem(z + 4, NZ))
-    for copy in across:
-        copy.wait_recv()
+    receive(across)
     q_store = pltpu.make_async_copy(all_q, q_out, load_sem.at[5])
     q_store.start()
     p_cat = jnp.concatenate([p_high, p_high, p_low], axis=0)
@@ -263,8 +267,10 @@
         store = pltpu.make_async_copy(err_v.at[:, cols], err_out.at[:, cols], load_sem.at[6 + t])
         store.start()
         stores.append(store)
-    for copy in unsent:
-        copy.wait_send()
+    for way in (1, -1):
+        for piece in flows[way][-2:]:
+            bulk[(way, *piece)].wait_send()
+    receive([])
     p_store.wait()
     q_store.wait()
     for store in stores:
@@ -281,7 +287,7 @@
             jax.ShapeDtypeStruct((8, 8, DOUT), F32),
             jax.ShapeDtypeStruct((FEAT, DOUT), BF16),
         ),
-        in_specs=[anywhere] * 4,
+        in_specs=[pl.BlockSpec(memory_space=pltpu.HBM)] * 4,
         out_specs=(anywhere,) * 3,
         scratch_shapes=[
             vmem(NZ, TOK, DOUT, dtype=BF16),
@@ -303,10 +309,10 @@
             pltpu.SemaphoreType.DMA((10,)),
         ],
         compiler_params=pltpu.CompilerParams(
-            collective_id=0, has_side_effects=True, vmem_limit_bytes=60 * 1024 * 1024
+            collective_id=0, has_side_effects=True, vmem_limit_bytes=48 * 1024 * 1024
         ),
         cost_estimate=pl.CostEstimate(flops=2 * 10**9, bytes_accessed=6 * 10**6, transcendentals=0),
-    )(x_input.reshape(NZ, TOK, FEAT), dy_grad[0], error_in[0], q_init.T)
+    )(*(pltpu.with_memory_space_constraint(v, pltpu.HBM) for v in (x_input.reshape(NZ, TOK, FEAT), dy_grad[0], error_in[0], q_init.T)))
     return p_t.T, q_t.reshape(RANK, DOUT).T, err[None]
 
 

time: 118 us -> 115 us (0.975)
  local copies, waits for them, and re-layouts: 4.41 us -> 2.39 us
    unnamed x5 -> x3, local copies, waits for them, and re-layouts: 4.41 us -> 2.39 us
where the time goes in v3:
time: 115 us
  Pallas kernels  112 us (97%)
  local copies, waits for them, and re-layouts  2.39 us (2%)
    pallas_call x1, Pallas kernels, local(): pl.pallas_call(kernel, out_shape=(jax.ShapeDtypeStruct((RANK, FEAT), F32)...  112 us
    unnamed x3, local copies, waits for them, and re-layouts  2.39 us

profile of v3, /device:TPU:1, one launch (start us, length us, event | category | flops | bytes accessed | tf_op | source)
XLA Modules:
  0.0 114.6 jit_solution(16399251771658371593)
XLA Ops:
  0.6 111.5 %shard_map.67 = (f32[64,256]{1,0:T(8,128)S(1)}, f32[8,8,2048]{2,1,0:T(8,128)S(1)}, bf16[256,2048]{1,0:T(8,128)(2,1)S(1)}) custom-call(bf16[8,192,256]{2,1,0:T(8,128)(2,1)} %bitcast.13, bf16[192,2048]{1,0:T(8,128)(2,1)} %bitcast.14, bf16[256,2048]{1,0:T(8,128)(2,1)} %bitcast.12, f32[64,2048]{1,0:T(8,128)} %bitcast.15), custom_call_target="tpu_custom_call" | custom-call | flops 2000000000 | bytes 6000000 | tf_op jit(solution)/shard_map/pallas_call | solution.py:283
  112.2 0.6 copy.10
  112.8 0.8 copy.11
  113.6 1.0 copy.12

commit v4 on v3

--- a/solution.py
+++ b/solution.py
@@ -107,10 +107,6 @@
     for peer in peers:
         pl.semaphore_signal(barrier, inc=1, device_id=peer, device_id_type=pl.DeviceIdType.MESH)
 
-    loads[0].wait()
-    loads[1].wait()
-    q_halves = jnp.concatenate(split_rows(qv[...]), axis=0)
-    yq[z] = split_lanes(mm(dyg[z], q_halves, NT))
     pl.semaphore_wait(barrier, len(peers))
 
     flows = {
@@ -122,7 +118,8 @@
     def bulk_send(way, hop, c):
         block = lax.rem(z - way * (hop - 1) + NZ, NZ)
         ref = dyg.at[block, pl.ds(c * PIECE, PIECE)]
-        bulk[way, hop, c] = send(ref, ref, at_z(way))
+        source = dy_ref.at[pl.ds(c * PIECE, PIECE)] if hop == 1 else ref
+        bulk[way, hop, c] = send(source, ref, at_z(way))
         unsent.pop()
 
     def bulk_forward(n):
@@ -140,17 +137,32 @@
             cols = pl.ds(pl.multiple_of(t * TILE, TILE), TILE)
             acc[:, cols] += mm(xv[block], dyg[block, :, cols], TN)
 
-    copies = [send(yq.at[z], yq.at[z], at_z(k)) for k in (4, 3, 5, 2, 6, 1, 7)]
-    for c in range(CHUNKS):
-        bulk_send(1, 1, c)
-        bulk_send(-1, 1, c)
+    bulk_send(1, 1, 0)
+    bulk_send(-1, 1, 0)
+    loads[0].wait()
+    loads[1].wait()
+    q_halves = jnp.concatenate(split_rows(qv[...]), axis=0)
+    yq[z] = split_lanes(mm(dyg[z], q_halves, NT))
+    right = send(yq.at[z], yq.at[z], at_z(1))
+    left = send(yq.at[z], yq.at[z], at_z(-1))
+    bulk_send(1, 1, 1)
+    bulk_send(-1, 1, 1)
     loads[2].wait()
     loads[3].wait()
     total = mm(q_halves, ev[...], NT) + mm(yq[z], xv[z], TN)
-    for k, copy in reversed(list(zip((4, 3, 5, 2, 6, 1, 7), copies))):
-        copy.wait_recv()
-        block = lax.rem(z - k + NZ, NZ)
-        total += mm(yq[block], xv[block], TN)
+    for hop in (1, 2, 3, 4):
+        from_left, from_right = lax.rem(z - hop + NZ, NZ), lax.rem(z + hop, NZ)
+        right.wait_recv()
+        if hop < 4:
+            right = send(yq.at[from_left], yq.at[from_left], at_z(1))
+            left.wait_recv()
+            if hop < 3:
+                left = send(yq.at[from_right], yq.at[from_right], at_z(-1))
+            if hop > 1:
+                bulk_send(1, 1, hop)
+                bulk_send(-1, 1, hop)
+            total += mm(yq[from_right], xv[from_right], TN)
+        total += mm(yq[from_left], xv[from_left], TN)
     total = total[:RANK] + total[RANK:]
 
     for k in range(NJ):
@@ -179,14 +191,12 @@
     in_g[z] = mm(all_p[j], p_twice, NT, HIGHEST)
     copies = [send(in_g.at[z], in_g.at[z], at_z(k)) for k in range(1, NZ)]
     bulk_forward(3)
-    add_grad(lax.rem(z + NZ - 1, NZ))
-    add_grad(lax.rem(z + 1, NZ))
     receive(copies)
     all_g[j] = sum(in_g[k] for k in range(1, NZ)) + in_g[0]
     copies = [send(all_g.at[j], all_g.at[j], at_j(k)) for k in range(1, NJ)]
     bulk_forward(4)
     receive(copies)
-    steps = {20: 5, 40: 6}
+    steps = {32: 5}
     between = lambda k: bulk_forward(steps[k]) if k in steps else None
     inverse = inverse_factor(all_g[...].reshape(RANK, 2 * RANK), between)
     p_t = mm(inverse, p_twice, NN, HIGHEST)
@@ -202,8 +212,9 @@
         block = lax.rem(z + k, NZ)
         part_x[block] = split_lanes(mm(xv[block], p_halves, NT))
         copies.append(send(part_x.at[block], in_x.at[z], at_z(k)))
+    bulk_forward(6)
     bulk_forward(7)
-    for hop in range(2, NEAR + 1):
+    for hop in range(1, NEAR + 1):
         add_grad(lax.rem(z + NZ - hop, NZ))
         add_grad(lax.rem(z + hop, NZ))
     receive(copies)
@@ -234,13 +245,9 @@
     in_qz[z] = sum(in_qy[k] for k in range(1, NY)) + in_qy[0]
     copies = [send(in_qz.at[z], in_qz.at[z], at_z(k)) for k in range(1, NZ)]
     bulk_forward(10)
-    bulk_forward(11)
     receive(copies)
     all_qy[y] = sum(in_qz[k] for k in range(1, NZ)) + in_qz[0]
     copies = [send(all_qy.at[y], all_qy.at[y], at_y(k)) for k in range(1, NY)]
-    for hop in range(NEAR + 1, 4):
-        add_grad(lax.rem(z + NZ - hop, NZ))
-        add_grad(lax.rem(z + hop, NZ))
     receive(copies)
     mine = core * NX + x
     for k in range(NY):
@@ -251,6 +258,10 @@
         copy.wait_recv()
         slot = core * NX + lax.rem(x - (k + 1) + NX, NX)
         across.append(send(all_q.at[slot], all_q.at[slot], at_core))
+    bulk_forward(11)
+    for hop in range(NEAR + 1, 4):
+        add_grad(lax.rem(z + NZ - hop, NZ))
+        add_grad(lax.rem(z + hop, NZ))
     bulk_forward(12)
     bulk_forward(13)
     add_grad(lax.rem(z + 4, NZ))

time: 115 us -> 112 us (0.974)
  Pallas kernels: 112 us -> 108 us
    pallas_call x1, Pallas kernels: 112 us -> 108 us  [local(): pl.pallas_call(kernel, out_shape=(jax.ShapeDtypeStruct((RANK, FEAT), F32)...]
where the time goes in v4:
time: 112 us; the launch traced here: 111 us
  Pallas kernels  108 us (96%)
  local copies, waits for them, and re-layouts  2.39 us (2%)
    pallas_call x1, Pallas kernels, local(): pl.pallas_call(kernel, out_shape=(jax.ShapeDtypeStruct((RANK, FEAT), F32)...  108 us
    unnamed x3, local copies, waits for them, and re-layouts  2.39 us

profile of v4, /device:TPU:1, one launch (start us, length us, event | category | flops | bytes accessed | tf_op | source)
XLA Modules:
  0.0 111.3 jit_solution(13260573777281099884)
XLA Ops:
  0.6 108.3 %shard_map.67 = (f32[64,256]{1,0:T(8,128)S(1)}, f32[8,8,2048]{2,1,0:T(8,128)S(1)}, bf16[256,2048]{1,0:T(8,128)(2,1)S(1)}) custom-call(bf16[8,192,256]{2,1,0:T(8,128)(2,1)} %bitcast.13, bf16[192,2048]{1,0:T(8,128)(2,1)} %bitcast.14, bf16[256,2048]{1,0:T(8,128)(2,1)} %bitcast.12, f32[64,2048]{1,0:T(8,128)} %bitcast.15), custom_call_target="tpu_custom_call" | custom-call | flops 2000000000 | bytes 6000000 | tf_op jit(solution)/shard_map/pallas_call | solution.py:294
  109.0 0.6 copy.10
  109.6 0.8 copy.11
  110.4 1.0 copy.12

commit v5 on v4

--- a/solution.py
+++ b/solution.py
@@ -64,7 +64,7 @@
 def kernel(
     x_ref, dy_ref, e_ref, q_ref, p_out, q_out, err_out,
     dyg, xv, ev, qv, yq, acc, part_p, in_pj, in_py, all_p, in_g, all_g, part_x, in_x,
-    q_part, in_qc, q_core, in_qx, q_y, in_qy, in_qz, all_qy, all_q, p_keep, err_v,
+    q_part, in_qc, q_core, in_qx, q_y, in_qy, in_qz, all_qy, all_q, p_keep,
     send_sem, recv_sem, load_sem,
 ):
     dp, z = lax.axis_index("dp"), lax.axis_index("mp")
@@ -111,7 +111,7 @@
 
     flows = {
         1: [(h, c) for h in (1, 2, 3) for c in range(CHUNKS)] + [(4, 0), (4, 1)],
-        -1: [(h, c) for h in (1, 2, 3) for c in range(CHUNKS)] + [(4, 2), (4, 3)],
+        -1: [(h, c) for h in (1, 2, 3) for c in (2, 3, 0, 1)] + [(4, 2), (4, 3)],
     }
     bulk = {}
 
@@ -121,6 +121,10 @@
         source = dy_ref.at[pl.ds(c * PIECE, PIECE)] if hop == 1 else ref
         bulk[way, hop, c] = send(source, ref, at_z(way))
         unsent.pop()
+
+    def first_sends(n):
+        for way in (1, -1):
+            bulk_send(way, *flows[way][n])
 
     def bulk_forward(n):
         for way in (1, -1):
@@ -137,16 +141,14 @@
             cols = pl.ds(pl.multiple_of(t * TILE, TILE), TILE)
             acc[:, cols] += mm(xv[block], dyg[block, :, cols], TN)
 
-    bulk_send(1, 1, 0)
-    bulk_send(-1, 1, 0)
+    first_sends(0)
     loads[0].wait()
     loads[1].wait()
     q_halves = jnp.concatenate(split_rows(qv[...]), axis=0)
     yq[z] = split_lanes(mm(dyg[z], q_halves, NT))
     right = send(yq.at[z], yq.at[z], at_z(1))
     left = send(yq.at[z], yq.at[z], at_z(-1))
-    bulk_send(1, 1, 1)
-    bulk_send(-1, 1, 1)
+    first_sends(1)
     loads[2].wait()
     loads[3].wait()
     total = mm(q_halves, ev[...], NT) + mm(yq[z], xv[z], TN)
@@ -159,8 +161,7 @@
             if hop < 3:
                 left = send(yq.at[from_right], yq.at[from_right], at_z(-1))
             if hop > 1:
-                bulk_send(1, 1, hop)
-                bulk_send(-1, 1, hop)
+                first_sends(hop)
             total += mm(yq[from_right], xv[from_right], TN)
         total += mm(yq[from_left], xv[from_left], TN)
     total = total[:RANK] + total[RANK:]
@@ -234,17 +235,16 @@
         q_core[k] = q_part[core, k] + in_qc[k]
     copies = [send(q_core.at[lax.rem(x + k, NX)], in_qx.at[x], at_x(k)) for k in range(1, NX)]
     in_qx[x] = q_core[x]
+    bulk_forward(9)
     receive(copies)
     rows = (in_qx[0] + in_qx[1]) + (in_qx[2] + in_qx[3])
     for k in range(NY):
         q_y[k] = rows[:, k * 256 : k * 256 + 256]
     copies = [send(q_y.at[lax.rem(y + k, NY)], in_qy.at[y], at_y(k)) for k in range(1, NY)]
     in_qy[y] = q_y[y]
-    bulk_forward(9)
     receive(copies)
     in_qz[z] = sum(in_qy[k] for k in range(1, NY)) + in_qy[0]
     copies = [send(in_qz.at[z], in_qz.at[z], at_z(k)) for k in range(1, NZ)]
-    bulk_forward(10)
     receive(copies)
     all_qy[y] = sum(in_qz[k] for k in range(1, NZ)) + in_qz[0]
     copies = [send(all_qy.at[y], all_qy.at[y], at_y(k)) for k in range(1, NY)]
@@ -258,34 +258,34 @@
         copy.wait_recv()
         slot = core * NX + lax.rem(x - (k + 1) + NX, NX)
         across.append(send(all_q.at[slot], all_q.at[slot], at_core))
+    receive(across)
+    q_store = pltpu.make_async_copy(all_q, q_out, load_sem.at[5])
+    q_store.start()
+    p_cat = jnp.concatenate([p_high, p_high, p_low], axis=0)
+
+    @pl.loop(0, DOUT // TILE)
+    def _(t):
+        cols = pl.ds(pl.multiple_of(t * TILE, TILE), TILE)
+        q_high, q_low = split_rows(all_q[:, :, cols].reshape(RANK, TILE))
+        acc[:, cols] -= mm(p_cat, jnp.concatenate([q_high, q_low, q_high], axis=0), TN)
+
+    bulk_forward(10)
     bulk_forward(11)
     for hop in range(NEAR + 1, 4):
         add_grad(lax.rem(z + NZ - hop, NZ))
         add_grad(lax.rem(z + hop, NZ))
     bulk_forward(12)
     bulk_forward(13)
-    add_grad(lax.rem(z + 4, NZ))
-    receive(across)
-    q_store = pltpu.make_async_copy(all_q, q_out, load_sem.at[5])
-    q_store.start()
-    p_cat = jnp.concatenate([p_high, p_high, p_low], axis=0)
-    stores = []
+    far = lax.rem(z + 4, NZ)
     for t in range(DOUT // TILE):
         cols = slice(t * TILE, t * TILE + TILE)
-        q_high, q_low = split_rows(all_q[:, :, cols].reshape(RANK, TILE))
-        approx = mm(p_cat, jnp.concatenate([q_high, q_low, q_high], axis=0), TN)
-        err_v[:, cols] = (acc[:, cols] - approx).astype(BF16)
-        store = pltpu.make_async_copy(err_v.at[:, cols], err_out.at[:, cols], load_sem.at[6 + t])
-        store.start()
-        stores.append(store)
+        err_out[:, cols] = (acc[:, cols] + mm(xv[far], dyg[far, :, cols], TN)).astype(BF16)
     for way in (1, -1):
         for piece in flows[way][-2:]:
             bulk[(way, *piece)].wait_send()
     receive([])
     p_store.wait()
     q_store.wait()
-    for store in stores:
-        store.wait()
 
 
 def local(x_input, dy_grad, error_in, q_init):
@@ -299,7 +299,7 @@
             jax.ShapeDtypeStruct((FEAT, DOUT), BF16),
         ),
         in_specs=[pl.BlockSpec(memory_space=pltpu.HBM)] * 4,
-        out_specs=(anywhere,) * 3,
+        out_specs=(anywhere, anywhere, pl.BlockSpec(memory_space=pltpu.VMEM)),
         scratch_shapes=[
             vmem(NZ, TOK, DOUT, dtype=BF16),
             vmem(NZ, TOK, FEAT, dtype=BF16),
@@ -314,10 +314,9 @@
             vmem(NY, 8, FEAT), vmem(NY, 8, FEAT), vmem(NZ, 8, FEAT), vmem(NY, 8, FEAT),
             vmem(8, 8, DOUT),
             vmem(RANK, FEAT),
-            vmem(FEAT, DOUT, dtype=BF16),
             pltpu.SemaphoreType.DMA((N_SEMS,)),
             pltpu.SemaphoreType.DMA((N_SEMS,)),
-            pltpu.SemaphoreType.DMA((10,)),
+            pltpu.SemaphoreType.DMA((6,)),
         ],
         compiler_params=pltpu.CompilerParams(
             collective_id=0, has_side_effects=True, vmem_limit_bytes=48 * 1024 * 1024

time: 112 us -> 114 us (1.018)
  Pallas kernels: 108 us -> 111 us
    pallas_call x1, Pallas kernels: 108 us -> 111 us  [local(): pl.pallas_call(kernel, out_shape=(jax.ShapeDtypeStruct((RANK, FEAT), F32)...]
where the time goes in v5:
time: 114 us
  Pallas kernels  111 us (97%)
  local copies, waits for them, and re-layouts  2.39 us (2%)
    pallas_call x1, Pallas kernels, local(): pl.pallas_call(kernel, out_shape=(jax.ShapeDtypeStruct((RANK, FEAT), F32)...  111 us
    unnamed x3, local copies, waits for them, and re-layouts  2.39 us

profile of v5, /device:TPU:1, one launch (start us, length us, event | category | flops | bytes accessed | tf_op | source)
XLA Modules:
  0.0 113.9 jit_solution(14349809947247294114)
XLA Ops:
  0.6 110.8 %shard_map.67 = (f32[64,256]{1,0:T(8,128)S(1)}, f32[8,8,2048]{2,1,0:T(8,128)S(1)}, bf16[256,2048]{1,0:T(8,128)(2,1)S(1)}) custom-call(bf16[8,192,256]{2,1,0:T(8,128)(2,1)} %bitcast.13, bf16[192,2048]{1,0:T(8,128)(2,1)} %bitcast.14, bf16[256,2048]{1,0:T(8,128)(2,1)} %bitcast.12, f32[64,2048]{1,0:T(8,128)} %bitcast.15), custom_call_target="tpu_custom_call" | custom-call | flops 2000000000 | bytes 6000000 | tf_op jit(solution)/shard_map/pallas_call | solution.py:294
  111.5 0.6 copy.10
  112.1 0.8 copy.11
  112.9 1.0 copy.12

commit v6 on v5

--- a/solution.py
+++ b/solution.py
@@ -14,6 +14,7 @@
 PIECE = TOK // CHUNKS
 TILE = 512
 PIVOTS = 4
+ORDER = (4, 3, 5, 2, 6, 1, 7)
 N_SEMS = 128
 NEAR = 2
 
@@ -64,7 +65,7 @@
 def kernel(
     x_ref, dy_ref, e_ref, q_ref, p_out, q_out, err_out,
     dyg, xv, ev, qv, yq, acc, part_p, in_pj, in_py, all_p, in_g, all_g, part_x, in_x,
-    q_part, in_qc, q_core, in_qx, q_y, in_qy, in_qz, all_qy, all_q, p_keep,
+    q_part, in_qc, q_core, in_qx, q_y, in_qy, in_qz, all_qy, all_q, p_keep, q_near,
     send_sem, recv_sem, load_sem,
 ):
     dp, z = lax.axis_index("dp"), lax.axis_index("mp")
@@ -168,7 +169,7 @@
 
     for k in range(NJ):
         part_p[k] = total[k * 8 : k * 8 + 8]
-    copies = [send(part_p.at[lax.rem(j + k, NJ)], in_pj.at[j], at_j(k)) for k in range(1, NJ)]
+    copies = [send(part_p.at[lax.rem(j + k, NJ)], in_pj.at[j], at_j(k)) for k in ORDER]
     in_pj[j] = part_p[j]
 
     @pl.loop(0, DOUT // TILE)
@@ -179,22 +180,24 @@
     bulk_forward(0)
     receive(copies)
     in_py[y] = sum(in_pj[k] for k in range(1, NJ)) + in_pj[0]
-    copies = [send(in_py.at[y], in_py.at[y], at_y(k)) for k in range(1, NY)]
+    copies = [send(in_py.at[y], in_py.at[y], at_y(k)) for k in ORDER]
     bulk_forward(1)
     receive(copies)
     all_p[j] = sum(in_py[k] for k in range(1, NY)) + in_py[0]
-    copies = [send(all_p.at[j], all_p.at[j], at_j(k)) for k in range(1, NJ)]
+    copies = [send(all_p.at[j], all_p.at[j], at_j(k)) for k in ORDER]
     bulk_forward(2)
     receive(copies)
     p_sum = all_p[...].reshape(RANK, FEAT)
     p_twice = jnp.concatenate([p_sum, p_sum], axis=0)
 
     in_g[z] = mm(all_p[j], p_twice, NT, HIGHEST)
-    copies = [send(in_g.at[z], in_g.at[z], at_z(k)) for k in range(1, NZ)]
+    copies = [send(in_g.at[z], in_g.at[z], at_z(k)) for k in ORDER]
     bulk_forward(3)
+    add_grad(lax.rem(z + NZ - 1, NZ))
+    add_grad(lax.rem(z + 1, NZ))
     receive(copies)
     all_g[j] = sum(in_g[k] for k in range(1, NZ)) + in_g[0]
-    copies = [send(all_g.at[j], all_g.at[j], at_j(k)) for k in range(1, NJ)]
+    copies = [send(all_g.at[j], all_g.at[j], at_j(k)) for k in ORDER]
     bulk_forward(4)
     receive(copies)
     steps = {32: 5}
@@ -207,7 +210,7 @@
     p_high, p_low = split_rows(p_t)
     p_halves = jnp.concatenate([p_high, p_low], axis=0)
 
-    far_steps = [k for k in (4, 3, 5, 2, 6, 1, 7) if min(k, NZ - k) > NEAR]
+    far_steps = [k for k in ORDER if min(k, NZ - k) > NEAR]
     copies = []
     for k in far_steps:
         block = lax.rem(z + k, NZ)
@@ -215,39 +218,46 @@
         copies.append(send(part_x.at[block], in_x.at[z], at_z(k)))
     bulk_forward(6)
     bulk_forward(7)
-    for hop in range(1, NEAR + 1):
+    for hop in range(2, NEAR + 1):
         add_grad(lax.rem(z + NZ - hop, NZ))
         add_grad(lax.rem(z + hop, NZ))
+
+    @pl.loop(0, DOUT // TILE)
+    def _(t):
+        cols = pl.ds(pl.multiple_of(t * TILE, TILE), TILE)
+        near_high, near_low = split_rows(acc[:, cols])
+        tile = mm(p_halves, near_high, NN)
+        q_near[:, cols] = tile[:RANK] + tile[RANK:] + mm(p_high, near_low, NN)
+
     receive(copies)
     xp = split_lanes(sum(in_x[lax.rem(z + NZ - k, NZ)].astype(F32) for k in far_steps))
-
+    copies = []
     for t in range(DOUT // TILE):
         cols = slice(t * TILE, t * TILE + TILE)
-        near_high, near_low = split_rows(acc[:, cols])
-        tile = mm(xp, dyg[z, :, cols], TN) + mm(p_halves, near_high, NN)
-        tile = tile[:RANK] + tile[RANK:] + mm(p_high, near_low, NN)
+        tile = mm(xp, dyg[z, :, cols], TN)
+        tile = tile[:RANK] + tile[RANK:] + q_near[:, cols]
         for k in range(8):
             q_part[k // 4, k % 4, :, cols] = tile[k * 8 : k * 8 + 8]
-    copy = send(q_part.at[1 - core], in_qc, at_core)
-    bulk_forward(8)
-    receive([copy])
+        copies.append(send(q_part.at[1 - core, :, :, cols], in_qc.at[:, :, cols], at_core))
+    receive(copies)
     for k in range(NX):
         q_core[k] = q_part[core, k] + in_qc[k]
     copies = [send(q_core.at[lax.rem(x + k, NX)], in_qx.at[x], at_x(k)) for k in range(1, NX)]
     in_qx[x] = q_core[x]
-    bulk_forward(9)
     receive(copies)
     rows = (in_qx[0] + in_qx[1]) + (in_qx[2] + in_qx[3])
     for k in range(NY):
         q_y[k] = rows[:, k * 256 : k * 256 + 256]
-    copies = [send(q_y.at[lax.rem(y + k, NY)], in_qy.at[y], at_y(k)) for k in range(1, NY)]
+    copies = [send(q_y.at[lax.rem(y + k, NY)], in_qy.at[y], at_y(k)) for k in ORDER]
     in_qy[y] = q_y[y]
+    bulk_forward(8)
     receive(copies)
     in_qz[z] = sum(in_qy[k] for k in range(1, NY)) + in_qy[0]
-    copies = [send(in_qz.at[z], in_qz.at[z], at_z(k)) for k in range(1, NZ)]
+    copies = [send(in_qz.at[z], in_qz.at[z], at_z(k)) for k in ORDER]
+    bulk_forward(9)
     receive(copies)
     all_qy[y] = sum(in_qz[k] for k in range(1, NZ)) + in_qz[0]
-    copies = [send(all_qy.at[y], all_qy.at[y], at_y(k)) for k in range(1, NY)]
+    copies = [send(all_qy.at[y], all_qy.at[y], at_y(k)) for k in ORDER]
     receive(copies)
     mine = core * NX + x
     for k in range(NY):
@@ -314,6 +324,7 @@
             vmem(NY, 8, FEAT), vmem(NY, 8, FEAT), vmem(NZ, 8, FEAT), vmem(NY, 8, FEAT),
             vmem(8, 8, DOUT),
             vmem(RANK, FEAT),
+            vmem(RANK, DOUT),
             pltpu.SemaphoreType.DMA((N_SEMS,)),
             pltpu.SemaphoreType.DMA((N_SEMS,)),
             pltpu.SemaphoreType.DMA((6,)),

time: 114 us -> 111 us (0.974)
  Pallas kernels: 111 us -> 108 us
    pallas_call x1, Pallas kernels: 111 us -> 108 us  [local(): pl.pallas_call(kernel, out_shape=(jax.ShapeDtypeStruct((RANK, FEAT), F32)...]
where the time goes in v6:
time: 111 us
  Pallas kernels  108 us (97%)
  local copies, waits for them, and re-layouts  2.39 us (2%)
    pallas_call x1, Pallas kernels, local(): pl.pallas_call(kernel, out_shape=(jax.ShapeDtypeStruct((RANK, FEAT), F32)...  108 us
    unnamed x3, local copies, waits for them, and re-layouts  2.39 us

profile of v6, /device:TPU:1, one launch (start us, length us, event | category | flops | bytes accessed | tf_op | source)
XLA Modules:
  0.0 111.2 jit_solution(3194087926951991347)
XLA Ops:
  0.6 108.2 %shard_map.67 = (f32[64,256]{1,0:T(8,128)S(1)}, f32[8,8,2048]{2,1,0:T(8,128)S(1)}, bf16[256,2048]{1,0:T(8,128)(2,1)S(1)}) custom-call(bf16[8,192,256]{2,1,0:T(8,128)(2,1)} %bitcast.13, bf16[192,2048]{1,0:T(8,128)(2,1)} %bitcast.14, bf16[256,2048]{1,0:T(8,128)(2,1)} %bitcast.12, f32[64,2048]{1,0:T(8,128)} %bitcast.15), custom_call_target="tpu_custom_call" | custom-call | flops 2000000000 | bytes 6000000 | tf_op jit(solution)/shard_map/pallas_call | solution.py:304
  108.8 0.6 copy.10
  109.4 0.8 copy.11
  110.2 1.0 copy.12

commit v7 on v6

--- a/solution.py
+++ b/solution.py
@@ -38,6 +38,18 @@
     high = both.astype(BF16).astype(F32)
     lane = lax.broadcasted_iota(jnp.int32, both.shape, 1)
     return jnp.where(lane < RANK, high, both - high).astype(BF16)
+
+
+def fold(twice):
+    half = RANK // 2
+    lane = lax.broadcasted_iota(jnp.int32, (half, 2 * RANK), 1)
+    return jnp.where(lane < RANK, twice[:half], twice[half:])
+
+
+def unfold(folded):
+    lane = lax.broadcasted_iota(jnp.int32, folded.shape, 1)
+    other = pltpu.roll(folded, RANK, axis=1)
+    return jnp.concatenate([jnp.where(lane < RANK, folded, other), jnp.where(lane < RANK, other, folded)], axis=0)
 
 
 def inverse_factor(gram2, between):
@@ -64,7 +76,7 @@
 
 def kernel(
     x_ref, dy_ref, e_ref, q_ref, p_out, q_out, err_out,
-    dyg, xv, ev, qv, yq, acc, part_p, in_pj, in_py, all_p, in_g, all_g, part_x, in_x,
+    dyg, xv, ev, qv, yq, acc, part_p, in_pj, in_py, all_p, in_g, part_x, in_x,
     q_part, in_qc, q_core, in_qx, q_y, in_qy, in_qz, all_qy, all_q, p_keep, q_near,
     send_sem, recv_sem, load_sem,
 ):
@@ -108,6 +120,10 @@
     for peer in peers:
         pl.semaphore_signal(barrier, inc=1, device_id=peer, device_id_type=pl.DeviceIdType.MESH)
 
+    loads[0].wait()
+    loads[1].wait()
+    q_halves = jnp.concatenate(split_rows(qv[...]), axis=0)
+    yq[z] = split_lanes(mm(dyg[z], q_halves, NT))
     pl.semaphore_wait(barrier, len(peers))
 
     flows = {
@@ -142,13 +158,9 @@
             cols = pl.ds(pl.multiple_of(t * TILE, TILE), TILE)
             acc[:, cols] += mm(xv[block], dyg[block, :, cols], TN)
 
-    first_sends(0)
-    loads[0].wait()
-    loads[1].wait()
-    q_halves = jnp.concatenate(split_rows(qv[...]), axis=0)
-    yq[z] = split_lanes(mm(dyg[z], q_halves, NT))
     right = send(yq.at[z], yq.at[z], at_z(1))
     left = send(yq.at[z], yq.at[z], at_z(-1))
+    first_sends(0)
     first_sends(1)
     loads[2].wait()
     loads[3].wait()
@@ -190,19 +202,16 @@
     p_sum = all_p[...].reshape(RANK, FEAT)
     p_twice = jnp.concatenate([p_sum, p_sum], axis=0)
 
-    in_g[z] = mm(all_p[j], p_twice, NT, HIGHEST)
+    in_g[z] = fold(mm(p_sum, p_twice, NT, HIGHEST))
     copies = [send(in_g.at[z], in_g.at[z], at_z(k)) for k in ORDER]
     bulk_forward(3)
     add_grad(lax.rem(z + NZ - 1, NZ))
     add_grad(lax.rem(z + 1, NZ))
     receive(copies)
-    all_g[j] = sum(in_g[k] for k in range(1, NZ)) + in_g[0]
-    copies = [send(all_g.at[j], all_g.at[j], at_j(k)) for k in ORDER]
-    bulk_forward(4)
-    receive(copies)
-    steps = {32: 5}
+    gram_twice = unfold(sum(in_g[k] for k in range(1, NZ)) + in_g[0])
+    steps = {24: 4, 52: 5}
     between = lambda k: bulk_forward(steps[k]) if k in steps else None
-    inverse = inverse_factor(all_g[...].reshape(RANK, 2 * RANK), between)
+    inverse = inverse_factor(gram_twice, between)
     p_t = mm(inverse, p_twice, NN, HIGHEST)
     p_keep[...] = p_t
     p_store = pltpu.make_async_copy(p_keep, p_out, load_sem.at[4])
@@ -242,7 +251,7 @@
     receive(copies)
     for k in range(NX):
         q_core[k] = q_part[core, k] + in_qc[k]
-    copies = [send(q_core.at[lax.rem(x + k, NX)], in_qx.at[x], at_x(k)) for k in range(1, NX)]
+    copies = [send(q_core.at[lax.rem(x + k, NX)], in_qx.at[x], at_x(k)) for k in (2, 1, 3)]
     in_qx[x] = q_core[x]
     receive(copies)
     rows = (in_qx[0] + in_qx[1]) + (in_qx[2] + in_qx[3])
@@ -262,34 +271,29 @@
     mine = core * NX + x
     for k in range(NY):
         all_q[mine, :, k * 256 : k * 256 + 256] = all_qy[k]
-    copies = [send(all_q.at[mine], all_q.at[mine], at_x(k)) for k in range(1, NX)]
+    copies = [send(all_q.at[mine], all_q.at[mine], at_x(k)) for k in (2, 1, 3)]
     across = [send(all_q.at[mine], all_q.at[mine], at_core)]
-    for k, copy in enumerate(copies):
+    for k, copy in ((1, copies[1]), (3, copies[2]), (2, copies[0])):
         copy.wait_recv()
-        slot = core * NX + lax.rem(x - (k + 1) + NX, NX)
+        slot = core * NX + lax.rem(x - k + NX, NX)
         across.append(send(all_q.at[slot], all_q.at[slot], at_core))
-    receive(across)
-    q_store = pltpu.make_async_copy(all_q, q_out, load_sem.at[5])
-    q_store.start()
-    p_cat = jnp.concatenate([p_high, p_high, p_low], axis=0)
-
-    @pl.loop(0, DOUT // TILE)
-    def _(t):
-        cols = pl.ds(pl.multiple_of(t * TILE, TILE), TILE)
-        q_high, q_low = split_rows(all_q[:, :, cols].reshape(RANK, TILE))
-        acc[:, cols] -= mm(p_cat, jnp.concatenate([q_high, q_low, q_high], axis=0), TN)
-
     bulk_forward(10)
     bulk_forward(11)
     for hop in range(NEAR + 1, 4):
         add_grad(lax.rem(z + NZ - hop, NZ))
         add_grad(lax.rem(z + hop, NZ))
+    receive(across)
+    q_store = pltpu.make_async_copy(all_q, q_out, load_sem.at[5])
+    q_store.start()
     bulk_forward(12)
     bulk_forward(13)
+    p_cat = jnp.concatenate([p_high, p_high, p_low], axis=0)
     far = lax.rem(z + 4, NZ)
     for t in range(DOUT // TILE):
         cols = slice(t * TILE, t * TILE + TILE)
-        err_out[:, cols] = (acc[:, cols] + mm(xv[far], dyg[far, :, cols], TN)).astype(BF16)
+        q_high, q_low = split_rows(all_q[:, :, cols].reshape(RANK, TILE))
+        approx = mm(p_cat, jnp.concatenate([q_high, q_low, q_high], axis=0), TN)
+        err_out[:, cols] = (acc[:, cols] + mm(xv[far], dyg[far, :, cols], TN) - approx).astype(BF16)
     for way in (1, -1):
         for piece in flows[way][-2:]:
             bulk[(way, *piece)].wait_send()
@@ -318,7 +322,7 @@
             vmem(NZ, TOK, 2 * RANK, dtype=BF16),
             vmem(FEAT, DOUT),
             vmem(NJ, 8, FEAT), vmem(NJ, 8, FEAT), vmem(NY, 8, FEAT), vmem(NJ, 8, FEAT),
-            vmem(NZ, 8, 2 * RANK), vmem(NJ, 8, 2 * RANK),
+            vmem(NZ, RANK // 2, 2 * RANK),
             vmem(NZ, TOK, 2 * RANK, dtype=BF16), vmem(NZ, TOK, 2 * RANK, dtype=BF16),
             vmem(2, NX, 8, DOUT), vmem(NX, 8, DOUT), vmem(NX, 8, DOUT), vmem(NX, 8, DOUT),
             vmem(NY, 8, FEAT), vmem(NY, 8, FEAT), vmem(NZ, 8, FEAT), vmem(NY, 8, FEAT),

time: 111 us -> 109 us (0.982)
  Pallas kernels: 108 us -> 106 us
    pallas_call x1, Pallas kernels: 108 us -> 106 us  [local(): pl.pallas_call(kernel, out_shape=(jax.ShapeDtypeStruct((RANK, FEAT), F32)...]
where the time goes in v7:
time: 109 us
  Pallas kernels  106 us (97%)
  local copies, waits for them, and re-layouts  2.39 us (2%)
    pallas_call x1, Pallas kernels, local(): pl.pallas_call(kernel, out_shape=(jax.ShapeDtypeStruct((RANK, FEAT), F32)...  106 us
    unnamed x3, local copies, waits for them, and re-layouts  2.39 us

profile of v7, /device:TPU:1, one launch (start us, length us, event | category | flops | bytes accessed | tf_op | source)
XLA Modules:
  0.0 108.6 jit_solution(5862902502185098905)
XLA Ops:
  0.6 105.6 %shard_map.67 = (f32[64,256]{1,0:T(8,128)S(1)}, f32[8,8,2048]{2,1,0:T(8,128)S(1)}, bf16[256,2048]{1,0:T(8,128)(2,1)S(1)}) custom-call(bf16[8,192,256]{2,1,0:T(8,128)(2,1)} %bitcast.13, bf16[192,2048]{1,0:T(8,128)(2,1)} %bitcast.14, bf16[256,2048]{1,0:T(8,128)(2,1)} %bitcast.12, f32[64,2048]{1,0:T(8,128)} %bitcast.15), custom_call_target="tpu_custom_call" | custom-call | flops 2000000000 | bytes 6000000 | tf_op jit(solution)/shard_map/pallas_call | solution.py:308
  106.2 0.6 copy.10
  106.9 0.8 copy.11
  107.7 1.0 copy.12

commit v8 on v7

--- a/solution.py
+++ b/solution.py
@@ -75,9 +75,9 @@
 
 
 def kernel(
-    x_ref, dy_ref, e_ref, q_ref, p_out, q_out, err_out,
-    dyg, xv, ev, qv, yq, acc, part_p, in_pj, in_py, all_p, in_g, part_x, in_x,
-    q_part, in_qc, q_core, in_qx, q_y, in_qy, in_qz, all_qy, all_q, p_keep, q_near,
+    x_ref, dy_ref, e_ref, q_ref, p_out, all_q, acc,
+    dyg, xv, ev, qv, yq, part_p, in_pj, in_py, all_p, in_g, part_x, in_x,
+    q_part, in_qc, q_core, in_qx, q_y, in_qy, in_qz, all_qy, q_near,
     send_sem, recv_sem, load_sem,
 ):
     dp, z = lax.axis_index("dp"), lax.axis_index("mp")
@@ -143,10 +143,15 @@
         for way in (1, -1):
             bulk_send(way, *flows[way][n])
 
-    def bulk_forward(n):
+    def bulk_wait(n):
+        for way in (1, -1):
+            bulk[(way, *flows[way][n])].wait_recv()
+
+    def bulk_forward(n, waited=False):
+        if not waited:
+            bulk_wait(n)
         for way in (1, -1):
             hop, c = flows[way][n]
-            bulk[way, hop, c].wait_recv()
             if (hop + 1, c) in flows[way]:
                 bulk_send(way, hop + 1, c)
             if n >= 2:
@@ -161,7 +166,6 @@
     right = send(yq.at[z], yq.at[z], at_z(1))
     left = send(yq.at[z], yq.at[z], at_z(-1))
     first_sends(0)
-    first_sends(1)
     loads[2].wait()
     loads[3].wait()
     total = mm(q_halves, ev[...], NT) + mm(yq[z], xv[z], TN)
@@ -174,7 +178,7 @@
             if hop < 3:
                 left = send(yq.at[from_right], yq.at[from_right], at_z(-1))
             if hop > 1:
-                first_sends(hop)
+                first_sends(hop - 1)
             total += mm(yq[from_right], xv[from_right], TN)
         total += mm(yq[from_left], xv[from_left], TN)
     total = total[:RANK] + total[RANK:]
@@ -183,6 +187,7 @@
         part_p[k] = total[k * 8 : k * 8 + 8]
     copies = [send(part_p.at[lax.rem(j + k, NJ)], in_pj.at[j], at_j(k)) for k in ORDER]
     in_pj[j] = part_p[j]
+    first_sends(3)
 
     @pl.loop(0, DOUT // TILE)
     def _(t):
@@ -213,9 +218,7 @@
     between = lambda k: bulk_forward(steps[k]) if k in steps else None
     inverse = inverse_factor(gram_twice, between)
     p_t = mm(inverse, p_twice, NN, HIGHEST)
-    p_keep[...] = p_t
-    p_store = pltpu.make_async_copy(p_keep, p_out, load_sem.at[4])
-    p_store.start()
+    p_out[...] = p_t
     p_high, p_low = split_rows(p_t)
     p_halves = jnp.concatenate([p_high, p_low], axis=0)
 
@@ -226,7 +229,7 @@
         part_x[block] = split_lanes(mm(xv[block], p_halves, NT))
         copies.append(send(part_x.at[block], in_x.at[z], at_z(k)))
     bulk_forward(6)
-    bulk_forward(7)
+    bulk_wait(7)
     for hop in range(2, NEAR + 1):
         add_grad(lax.rem(z + NZ - hop, NZ))
         add_grad(lax.rem(z + hop, NZ))
@@ -239,6 +242,7 @@
         q_near[:, cols] = tile[:RANK] + tile[RANK:] + mm(p_high, near_low, NN)
 
     receive(copies)
+    bulk_forward(7, waited=True)
     xp = split_lanes(sum(in_x[lax.rem(z + NZ - k, NZ)].astype(F32) for k in far_steps))
     copies = []
     for t in range(DOUT // TILE):
@@ -248,22 +252,22 @@
         for k in range(8):
             q_part[k // 4, k % 4, :, cols] = tile[k * 8 : k * 8 + 8]
         copies.append(send(q_part.at[1 - core, :, :, cols], in_qc.at[:, :, cols], at_core))
+    bulk_forward(8)
     receive(copies)
     for k in range(NX):
         q_core[k] = q_part[core, k] + in_qc[k]
     copies = [send(q_core.at[lax.rem(x + k, NX)], in_qx.at[x], at_x(k)) for k in (2, 1, 3)]
     in_qx[x] = q_core[x]
+    bulk_forward(9)
     receive(copies)
     rows = (in_qx[0] + in_qx[1]) + (in_qx[2] + in_qx[3])
     for k in range(NY):
         q_y[k] = rows[:, k * 256 : k * 256 + 256]
     copies = [send(q_y.at[lax.rem(y + k, NY)], in_qy.at[y], at_y(k)) for k in ORDER]
     in_qy[y] = q_y[y]
-    bulk_forward(8)
     receive(copies)
     in_qz[z] = sum(in_qy[k] for k in range(1, NY)) + in_qy[0]
     copies = [send(in_qz.at[z], in_qz.at[z], at_z(k)) for k in ORDER]
-    bulk_forward(9)
     receive(copies)
     all_qy[y] = sum(in_qz[k] for k in range(1, NZ)) + in_qz[0]
     copies = [send(all_qy.at[y], all_qy.at[y], at_y(k)) for k in ORDER]
@@ -282,62 +286,78 @@
     for hop in range(NEAR + 1, 4):
         add_grad(lax.rem(z + NZ - hop, NZ))
         add_grad(lax.rem(z + hop, NZ))
-    receive(across)
-    q_store = pltpu.make_async_copy(all_q, q_out, load_sem.at[5])
-    q_store.start()
     bulk_forward(12)
     bulk_forward(13)
-    p_cat = jnp.concatenate([p_high, p_high, p_low], axis=0)
-    far = lax.rem(z + 4, NZ)
-    for t in range(DOUT // TILE):
-        cols = slice(t * TILE, t * TILE + TILE)
-        q_high, q_low = split_rows(all_q[:, :, cols].reshape(RANK, TILE))
-        approx = mm(p_cat, jnp.concatenate([q_high, q_low, q_high], axis=0), TN)
-        err_out[:, cols] = (acc[:, cols] + mm(xv[far], dyg[far, :, cols], TN) - approx).astype(BF16)
+    add_grad(lax.rem(z + 4, NZ))
+    receive(across)
     for way in (1, -1):
         for piece in flows[way][-2:]:
             bulk[(way, *piece)].wait_send()
     receive([])
-    p_store.wait()
-    q_store.wait()
+
+
+def finish(acc, p_ref, q_ref, p_out, q_out, err_out, err_v, sem):
+    copies = [pltpu.make_async_copy(p_ref, p_out, sem.at[0]), pltpu.make_async_copy(q_ref, q_out, sem.at[1])]
+    for copy in copies:
+        copy.start()
+    p_high, p_low = split_rows(p_ref[...])
+    p_cat = jnp.concatenate([p_high, p_high, p_low], axis=0)
+    for t in range(DOUT // TILE):
+        cols = slice(t * TILE, t * TILE + TILE)
+        q_high, q_low = split_rows(q_ref[:, :, cols].reshape(RANK, TILE))
+        approx = mm(p_cat, jnp.concatenate([q_high, q_low, q_high], axis=0), TN)
+        err_v[:, cols] = (acc[:, cols] - approx).astype(BF16)
+        copy = pltpu.make_async_copy(err_v.at[:, cols], err_out.at[:, cols], sem.at[2 + t])
+        copy.start()
+        copies.append(copy)
+    for copy in copies:
+        copy.wait()
 
 
 def local(x_input, dy_grad, error_in, q_init):
     anywhere = pl.BlockSpec(memory_space=pl.ANY)
     vmem = lambda *shape, dtype=F32: pltpu.VMEM(shape, dtype)
-    p_t, q_t, err = pl.pallas_call(
+    shapes = (
+        jax.ShapeDtypeStruct((RANK, FEAT), F32),
+        jax.ShapeDtypeStruct((8, 8, DOUT), F32),
+        jax.ShapeDtypeStruct((FEAT, DOUT), F32),
+    )
+    held = [pl.BlockSpec(memory_space=pltpu.VMEM)] * 3
+    p_t, q_t, acc = pl.pallas_call(
         kernel,
-        out_shape=(
-            jax.ShapeDtypeStruct((RANK, FEAT), F32),
-            jax.ShapeDtypeStruct((8, 8, DOUT), F32),
-            jax.ShapeDtypeStruct((FEAT, DOUT), BF16),
-        ),
+        out_shape=shapes,
         in_specs=[pl.BlockSpec(memory_space=pltpu.HBM)] * 4,
-        out_specs=(anywhere, anywhere, pl.BlockSpec(memory_space=pltpu.VMEM)),
+        out_specs=held,
         scratch_shapes=[
             vmem(NZ, TOK, DOUT, dtype=BF16),
             vmem(NZ, TOK, FEAT, dtype=BF16),
             vmem(FEAT, DOUT, dtype=BF16),
             vmem(RANK, DOUT),
             vmem(NZ, TOK, 2 * RANK, dtype=BF16),
-            vmem(FEAT, DOUT),
             vmem(NJ, 8, FEAT), vmem(NJ, 8, FEAT), vmem(NY, 8, FEAT), vmem(NJ, 8, FEAT),
             vmem(NZ, RANK // 2, 2 * RANK),
             vmem(NZ, TOK, 2 * RANK, dtype=BF16), vmem(NZ, TOK, 2 * RANK, dtype=BF16),
             vmem(2, NX, 8, DOUT), vmem(NX, 8, DOUT), vmem(NX, 8, DOUT), vmem(NX, 8, DOUT),
             vmem(NY, 8, FEAT), vmem(NY, 8, FEAT), vmem(NZ, 8, FEAT), vmem(NY, 8, FEAT),
-            vmem(8, 8, DOUT),
-            vmem(RANK, FEAT),
             vmem(RANK, DOUT),
             pltpu.SemaphoreType.DMA((N_SEMS,)),
             pltpu.SemaphoreType.DMA((N_SEMS,)),
-            pltpu.SemaphoreType.DMA((6,)),
+            pltpu.SemaphoreType.DMA((4,)),
         ],
         compiler_params=pltpu.CompilerParams(
             collective_id=0, has_side_effects=True, vmem_limit_bytes=48 * 1024 * 1024
         ),
         cost_estimate=pl.CostEstimate(flops=2 * 10**9, bytes_accessed=6 * 10**6, transcendentals=0),
     )(*(pltpu.with_memory_space_constraint(v, pltpu.HBM) for v in (x_input.reshape(NZ, TOK, FEAT), dy_grad[0], error_in[0], q_init.T)))
+    p_t, q_t, err = pl.pallas_call(
+        finish,
+        out_shape=(*shapes[:2], jax.ShapeDtypeStruct((FEAT, DOUT), BF16)),
+        in_specs=held,
+        out_specs=[anywhere] * 3,
+        scratch_shapes=[vmem(FEAT, DOUT, dtype=BF16), pltpu.SemaphoreType.DMA((2 + DOUT // TILE,))],
+        compiler_params=pltpu.CompilerParams(vmem_limit_bytes=16 * 1024 * 1024),
+        cost_estimate=pl.CostEstimate(flops=2 * 10**8, bytes_accessed=2 * 10**6, transcendentals=0),
+    )(acc, p_t, q_t)
     return p_t.T, q_t.reshape(RANK, DOUT).T, err[None]
 
 

time: 109 us -> 108 us (level)
  local copies, waits for them, and re-layouts: 2.39 us -> 0 us
    unnamed x3 -> x0, local copies, waits for them, and re-layouts: 2.39 us -> none
    pallas_call x1 -> x2, Pallas kernels: 106 us -> 107 us  [the longest x1 106 us: local(): pl.pallas_call(kernel, out_shape=shapes, in_specs=[pl.BlockSpec(memory_sp...]
where the time goes in v8:
time: 108 us
  Pallas kernels  107 us (99%)
    pallas_call x1, Pallas kernels, local(): pl.pallas_call(kernel, out_shape=shapes, in_specs=[pl.BlockSpec(memory_sp...  106 us

profile of v8, /device:TPU:1, one launch (start us, length us, event | category | flops | bytes accessed | tf_op | source)
XLA Modules:
  0.0 108.0 jit_solution(4749020258206723248)
XLA Ops:
  0.6 106.1 %shard_map.67 = (f32[64,256]{1,0:T(8,128)S(1)}, f32[8,8,2048]{2,1,0:T(8,128)S(1)}, f32[256,2048]{1,0:T(8,128)S(1)}) custom-call(bf16[8,192,256]{2,1,0:T(8,128)(2,1)} %bitcast.11, bf16[192,2048]{1,0:T(8,128)(2,1)} %bitcast.12, bf16[256,2048]{1,0:T(8,128)(2,1)} %bitcast.9, f32[64,2048]{1,0:T(8,128)} %bitcast.13), custom_call_target="tpu_custom_call" | custom-call | flops 2000000000 | bytes 6000000 | tf_op jit(solution)/shard_map/pallas_call | solution.py:326
  106.8 1.3 %shard_map.68 = (f32[64,256]{1,0:T(8,128)}, f32[8,8,2048]{2,1,0:T(8,128)}, bf16[256,2048]{1,0:T(8,128)(2,1)}) custom-call(f32[256,2048]{1,0:T(8,128)S(1)} %get-tuple-element.9.acc, f32[64,256]{1,0:T(8,128)S(1)} %get-tuple-element.10.p_ref, f32[8,8,2048]{2,1,0:T(8,128)S(1)} %get-tuple-element.11.q_ref), custom_call_target="tpu_custom_call" | custom-call | flops 200000000 | bytes 2000000 | tf_op jit(solution)/shard_map/pallas_call | solution.py:352

commit v9 on v8

--- a/solution.py
+++ b/solution.py
@@ -38,18 +38,6 @@
     high = both.astype(BF16).astype(F32)
     lane = lax.broadcasted_iota(jnp.int32, both.shape, 1)
     return jnp.where(lane < RANK, high, both - high).astype(BF16)
-
-
-def fold(twice):
-    half = RANK // 2
-    lane = lax.broadcasted_iota(jnp.int32, (half, 2 * RANK), 1)
-    return jnp.where(lane < RANK, twice[:half], twice[half:])
-
-
-def unfold(folded):
-    lane = lax.broadcasted_iota(jnp.int32, folded.shape, 1)
-    other = pltpu.roll(folded, RANK, axis=1)
-    return jnp.concatenate([jnp.where(lane < RANK, folded, other), jnp.where(lane < RANK, other, folded)], axis=0)
 
 
 def inverse_factor(gram2, between):
@@ -76,7 +64,7 @@
 
 def kernel(
     x_ref, dy_ref, e_ref, q_ref, p_out, all_q, acc,
-    dyg, xv, ev, qv, yq, part_p, in_pj, in_py, all_p, in_g, part_x, in_x,
+    dyg, xv, ev, qv, yq, part_p, in_pj, in_py, all_p, in_g, all_g, part_x, in_x,
     q_part, in_qc, q_core, in_qx, q_y, in_qy, in_qz, all_qy, q_near,
     send_sem, recv_sem, load_sem,
 ):
@@ -120,10 +108,6 @@
     for peer in peers:
         pl.semaphore_signal(barrier, inc=1, device_id=peer, device_id_type=pl.DeviceIdType.MESH)
 
-    loads[0].wait()
-    loads[1].wait()
-    q_halves = jnp.concatenate(split_rows(qv[...]), axis=0)
-    yq[z] = split_lanes(mm(dyg[z], q_halves, NT))
     pl.semaphore_wait(barrier, len(peers))
 
     flows = {
@@ -143,15 +127,10 @@
         for way in (1, -1):
             bulk_send(way, *flows[way][n])
 
-    def bulk_wait(n):
-        for way in (1, -1):
-            bulk[(way, *flows[way][n])].wait_recv()
-
-    def bulk_forward(n, waited=False):
-        if not waited:
-            bulk_wait(n)
+    def bulk_forward(n):
         for way in (1, -1):
             hop, c = flows[way][n]
+            bulk[way, hop, c].wait_recv()
             if (hop + 1, c) in flows[way]:
                 bulk_send(way, hop + 1, c)
             if n >= 2:
@@ -163,9 +142,14 @@
             cols = pl.ds(pl.multiple_of(t * TILE, TILE), TILE)
             acc[:, cols] += mm(xv[block], dyg[block, :, cols], TN)
 
+    first_sends(0)
+    loads[0].wait()
+    loads[1].wait()
+    q_halves = jnp.concatenate(split_rows(qv[...]), axis=0)
+    yq[z] = split_lanes(mm(dyg[z], q_halves, NT))
     right = send(yq.at[z], yq.at[z], at_z(1))
     left = send(yq.at[z], yq.at[z], at_z(-1))
-    first_sends(0)
+    first_sends(1)
     loads[2].wait()
     loads[3].wait()
     total = mm(q_halves, ev[...], NT) + mm(yq[z], xv[z], TN)
@@ -178,7 +162,7 @@
             if hop < 3:
                 left = send(yq.at[from_right], yq.at[from_right], at_z(-1))
             if hop > 1:
-                first_sends(hop - 1)
+                first_sends(hop)
             total += mm(yq[from_right], xv[from_right], TN)
         total += mm(yq[from_left], xv[from_left], TN)
     total = total[:RANK] + total[RANK:]
@@ -187,7 +171,6 @@
         part_p[k] = total[k * 8 : k * 8 + 8]
     copies = [send(part_p.at[lax.rem(j + k, NJ)], in_pj.at[j], at_j(k)) for k in ORDER]
     in_pj[j] = part_p[j]
-    first_sends(3)
 
     @pl.loop(0, DOUT // TILE)
     def _(t):
@@ -207,16 +190,19 @@
     p_sum = all_p[...].reshape(RANK, FEAT)
     p_twice = jnp.concatenate([p_sum, p_sum], axis=0)
 
-    in_g[z] = fold(mm(p_sum, p_twice, NT, HIGHEST))
+    in_g[z] = mm(all_p[j], p_twice, NT, HIGHEST)
     copies = [send(in_g.at[z], in_g.at[z], at_z(k)) for k in ORDER]
     bulk_forward(3)
     add_grad(lax.rem(z + NZ - 1, NZ))
     add_grad(lax.rem(z + 1, NZ))
     receive(copies)
-    gram_twice = unfold(sum(in_g[k] for k in range(1, NZ)) + in_g[0])
-    steps = {24: 4, 52: 5}
+    all_g[j] = sum(in_g[k] for k in range(1, NZ)) + in_g[0]
+    copies = [send(all_g.at[j], all_g.at[j], at_j(k)) for k in ORDER]
+    bulk_forward(4)
+    receive(copies)
+    steps = {32: 5}
     between = lambda k: bulk_forward(steps[k]) if k in steps else None
-    inverse = inverse_factor(gram_twice, between)
+    inverse = inverse_factor(all_g[...].reshape(RANK, 2 * RANK), between)
     p_t = mm(inverse, p_twice, NN, HIGHEST)
     p_out[...] = p_t
     p_high, p_low = split_rows(p_t)
@@ -229,7 +215,7 @@
         part_x[block] = split_lanes(mm(xv[block], p_halves, NT))
         copies.append(send(part_x.at[block], in_x.at[z], at_z(k)))
     bulk_forward(6)
-    bulk_wait(7)
+    bulk_forward(7)
     for hop in range(2, NEAR + 1):
         add_grad(lax.rem(z + NZ - hop, NZ))
         add_grad(lax.rem(z + hop, NZ))
@@ -242,7 +228,7 @@
         q_near[:, cols] = tile[:RANK] + tile[RANK:] + mm(p_high, near_low, NN)
 
     receive(copies)
-    bulk_forward(7, waited=True)
+    bulk_forward(8)
     xp = split_lanes(sum(in_x[lax.rem(z + NZ - k, NZ)].astype(F32) for k in far_steps))
     copies = []
     for t in range(DOUT // TILE):
@@ -252,7 +238,6 @@
         for k in range(8):
             q_part[k // 4, k % 4, :, cols] = tile[k * 8 : k * 8 + 8]
         copies.append(send(q_part.at[1 - core, :, :, cols], in_qc.at[:, :, cols], at_core))
-    bulk_forward(8)
     receive(copies)
     for k in range(NX):
         q_core[k] = q_part[core, k] + in_qc[k]
@@ -335,7 +320,7 @@
             vmem(RANK, DOUT),
             vmem(NZ, TOK, 2 * RANK, dtype=BF16),
             vmem(NJ, 8, FEAT), vmem(NJ, 8, FEAT), vmem(NY, 8, FEAT), vmem(NJ, 8, FEAT),
-            vmem(NZ, RANK // 2, 2 * RANK),
+            vmem(NZ, 8, 2 * RANK), vmem(NJ, 8, 2 * RANK),
             vmem(NZ, TOK, 2 * RANK, dtype=BF16), vmem(NZ, TOK, 2 * RANK, dtype=BF16),
             vmem(2, NX, 8, DOUT), vmem(NX, 8, DOUT), vmem(NX, 8, DOUT), vmem(NX, 8, DOUT),
             vmem(NY, 8, FEAT), vmem(NY, 8, FEAT), vmem(NZ, 8, FEAT), vmem(NY, 8, FEAT),

time: 108 us -> 108 us (level)
  no operation moved by 1% of the time
where the time goes in v9:
time: 108 us
  Pallas kernels  107 us (99%)
    pallas_call x1, Pallas kernels, local(): pl.pallas_call(kernel, out_shape=shapes, in_specs=[pl.BlockSpec(memory_sp...  106 us

profile of v9, /device:TPU:1, one launch (start us, length us, event | category | flops | bytes accessed | tf_op | source)
XLA Modules:
  0.0 108.1 jit_solution(8402338773011730712)
XLA Ops:
  0.6 106.1 %shard_map.67 = (f32[64,256]{1,0:T(8,128)S(1)}, f32[8,8,2048]{2,1,0:T(8,128)S(1)}, f32[256,2048]{1,0:T(8,128)S(1)}) custom-call(bf16[8,192,256]{2,1,0:T(8,128)(2,1)} %bitcast.11, bf16[192,2048]{1,0:T(8,128)(2,1)} %bitcast.12, bf16[256,2048]{1,0:T(8,128)(2,1)} %bitcast.9, f32[64,2048]{1,0:T(8,128)} %bitcast.13), custom_call_target="tpu_custom_call" | custom-call | flops 2000000000 | bytes 6000000 | tf_op jit(solution)/shard_map/pallas_call | solution.py:311
  106.8 1.3 %shard_map.68 = (f32[64,256]{1,0:T(8,128)}, f32[8,8,2048]{2,1,0:T(8,128)}, bf16[256,2048]{1,0:T(8,128)(2,1)}) custom-call(f32[256,2048]{1,0:T(8,128)S(1)} %get-tuple-element.9.acc, f32[64,256]{1,0:T(8,128)S(1)} %get-tuple-element.10.p_ref, f32[8,8,2048]{2,1,0:T(8,128)S(1)} %get-tuple-element.11.q_ref), custom_call_target="tpu_custom_call" | custom-call | flops 200000000 | bytes 2000000 | tf_op jit(solution)/shard_map/pallas_call | solution.py:337

commit v10 on v9

--- a/solution.py
+++ b/solution.py
@@ -208,12 +208,17 @@
     p_high, p_low = split_rows(p_t)
     p_halves = jnp.concatenate([p_high, p_low], axis=0)
 
-    far_steps = [k for k in ORDER if min(k, NZ - k) > NEAR]
-    copies = []
-    for k in far_steps:
-        block = lax.rem(z + k, NZ)
-        part_x[block] = split_lanes(mm(xv[block], p_halves, NT))
-        copies.append(send(part_x.at[block], in_x.at[z], at_z(k)))
+    block = lax.rem(z + 4, NZ)
+    part_x[0] = split_lanes(mm(xv[block], p_halves, NT))
+    relay = send(part_x.at[0], in_x.at[2], at_z(-1))
+    block = lax.rem(z + 3, NZ)
+    part_x[1] = split_lanes(mm(xv[block], p_halves, NT))
+    copies = [send(part_x.at[1], in_x.at[0], at_z(3))]
+    block = lax.rem(z + 5, NZ)
+    own_part = mm(xv[block], p_halves, NT)
+    relay.wait_recv()
+    part_x[2] = split_lanes(own_part + in_x[2].astype(F32))
+    copies.append(send(part_x.at[2], in_x.at[1], at_z(5)))
     bulk_forward(6)
     bulk_forward(7)
     for hop in range(2, NEAR + 1):
@@ -229,7 +234,7 @@
 
     receive(copies)
     bulk_forward(8)
-    xp = split_lanes(sum(in_x[lax.rem(z + NZ - k, NZ)].astype(F32) for k in far_steps))
+    xp = split_lanes(in_x[0].astype(F32) + in_x[1].astype(F32))
     copies = []
     for t in range(DOUT // TILE):
         cols = slice(t * TILE, t * TILE + TILE)
@@ -321,7 +326,7 @@
             vmem(NZ, TOK, 2 * RANK, dtype=BF16),
             vmem(NJ, 8, FEAT), vmem(NJ, 8, FEAT), vmem(NY, 8, FEAT), vmem(NJ, 8, FEAT),
             vmem(NZ, 8, 2 * RANK), vmem(NJ, 8, 2 * RANK),
-            vmem(NZ, TOK, 2 * RANK, dtype=BF16), vmem(NZ, TOK, 2 * RANK, dtype=BF16),
+            vmem(3, TOK, 2 * RANK, dtype=BF16), vmem(3, TOK, 2 * RANK, dtype=BF16),
             vmem(2, NX, 8, DOUT), vmem(NX, 8, DOUT), vmem(NX, 8, DOUT), vmem(NX, 8, DOUT),
             vmem(NY, 8, FEAT), vmem(NY, 8, FEAT), vmem(NZ, 8, FEAT), vmem(NY, 8, FEAT),
             vmem(RANK, DOUT),

time: 108 us -> 107 us (level)
  no operation moved by 1% of the time
where the time goes in v10:
time: 107 us
  Pallas kernels  107 us (100%)
    pallas_call x1, Pallas kernels, local(): pl.pallas_call(kernel, out_shape=shapes, in_specs=[pl.BlockSpec(memory_sp...  105 us

profile of v10, /device:TPU:1, one launch (start us, length us, event | category | flops | bytes accessed | tf_op | source)
XLA Modules:
  0.0 107.2 jit_solution(12472767687847288868)
XLA Ops:
  0.6 105.3 %shard_map.67 = (f32[64,256]{1,0:T(8,128)S(1)}, f32[8,8,2048]{2,1,0:T(8,128)S(1)}, f32[256,2048]{1,0:T(8,128)S(1)}) custom-call(bf16[8,192,256]{2,1,0:T(8,128)(2,1)} %bitcast.11, bf16[192,2048]{1,0:T(8,128)(2,1)} %bitcast.12, bf16[256,2048]{1,0:T(8,128)(2,1)} %bitcast.9, f32[64,2048]{1,0:T(8,128)} %bitcast.13), custom_call_target="tpu_custom_call" | custom-call | flops 2000000000 | bytes 6000000 | tf_op jit(solution)/shard_map/pallas_call | solution.py:316
  106.0 1.3 %shard_map.68 = (f32[64,256]{1,0:T(8,128)}, f32[8,8,2048]{2,1,0:T(8,128)}, bf16[256,2048]{1,0:T(8,128)(2,1)}) custom-call(f32[256,2048]{1,0:T(8,128)S(1)} %get-tuple-element.9.acc, f32[64,256]{1,0:T(8,128)S(1)} %get-tuple-element.10.p_ref, f32[8,8,2048]{2,1,0:T(8,128)S(1)} %get-tuple-element.11.q_ref), custom_call_target="tpu_custom_call" | custom-call | flops 200000000 | bytes 2000000 | tf_op jit(solution)/shard_map/pallas_call | solution.py:342

commit v11 on v10

--- a/solution.py
+++ b/solution.py
@@ -216,10 +216,10 @@
     copies = [send(part_x.at[1], in_x.at[0], at_z(3))]
     block = lax.rem(z + 5, NZ)
     own_part = mm(xv[block], p_halves, NT)
+    bulk_forward(6)
     relay.wait_recv()
     part_x[2] = split_lanes(own_part + in_x[2].astype(F32))
     copies.append(send(part_x.at[2], in_x.at[1], at_z(5)))
-    bulk_forward(6)
     bulk_forward(7)
     for hop in range(2, NEAR + 1):
         add_grad(lax.rem(z + NZ - hop, NZ))

time: 107 us -> 108 us (level)
  no operation moved by 1% of the time
where the time goes in v11:
time: 108 us; the launch traced here: 107 us
  Pallas kernels  107 us (99%)
    pallas_call x1, Pallas kernels, local(): pl.pallas_call(kernel, out_shape=shapes, in_specs=[pl.BlockSpec(memory_sp...  106 us

profile of v11, /device:TPU:1, one launch (start us, length us, event | category | flops | bytes accessed | tf_op | source)
XLA Modules:
  0.0 107.4 jit_solution(3336607379074010875)
XLA Ops:
  0.6 105.5 %shard_map.67 = (f32[64,256]{1,0:T(8,128)S(1)}, f32[8,8,2048]{2,1,0:T(8,128)S(1)}, f32[256,2048]{1,0:T(8,128)S(1)}) custom-call(bf16[8,192,256]{2,1,0:T(8,128)(2,1)} %bitcast.11, bf16[192,2048]{1,0:T(8,128)(2,1)} %bitcast.12, bf16[256,2048]{1,0:T(8,128)(2,1)} %bitcast.9, f32[64,2048]{1,0:T(8,128)} %bitcast.13), custom_call_target="tpu_custom_call" | custom-call | flops 2000000000 | bytes 6000000 | tf_op jit(solution)/shard_map/pallas_call | solution.py:316
  106.1 1.3 %shard_map.68 = (f32[64,256]{1,0:T(8,128)}, f32[8,8,2048]{2,1,0:T(8,128)}, bf16[256,2048]{1,0:T(8,128)(2,1)}) custom-call(f32[256,2048]{1,0:T(8,128)S(1)} %get-tuple-element.9.acc, f32[64,256]{1,0:T(8,128)S(1)} %get-tuple-element.10.p_ref, f32[8,8,2048]{2,1,0:T(8,128)S(1)} %get-tuple-element.11.q_ref), custom_call_target="tpu_custom_call" | custom-call | flops 200000000 | bytes 2000000 | tf_op jit(solution)/shard_map/pallas_call | solution.py:342

commit v12 on v11

--- a/solution.py
+++ b/solution.py
@@ -243,12 +243,12 @@
         for k in range(8):
             q_part[k // 4, k % 4, :, cols] = tile[k * 8 : k * 8 + 8]
         copies.append(send(q_part.at[1 - core, :, :, cols], in_qc.at[:, :, cols], at_core))
+    bulk_forward(9)
     receive(copies)
     for k in range(NX):
         q_core[k] = q_part[core, k] + in_qc[k]
     copies = [send(q_core.at[lax.rem(x + k, NX)], in_qx.at[x], at_x(k)) for k in (2, 1, 3)]
     in_qx[x] = q_core[x]
-    bulk_forward(9)
     receive(copies)
     rows = (in_qx[0] + in_qx[1]) + (in_qx[2] + in_qx[3])
     for k in range(NY):

time: 108 us -> 108 us (level)
  no operation moved by 1% of the time
where the time goes in v12:
time: 108 us; the launch traced here: 107 us
  Pallas kernels  107 us (99%)
    pallas_call x1, Pallas kernels, local(): pl.pallas_call(kernel, out_shape=shapes, in_specs=[pl.BlockSpec(memory_sp...  106 us

profile of v12, /device:TPU:1, one launch (start us, length us, event | category | flops | bytes accessed | tf_op | source)
XLA Modules:
  0.0 107.4 jit_solution(5479951137139003502)
XLA Ops:
  0.6 105.5 %shard_map.67 = (f32[64,256]{1,0:T(8,128)S(1)}, f32[8,8,2048]{2,1,0:T(8,128)S(1)}, f32[256,2048]{1,0:T(8,128)S(1)}) custom-call(bf16[8,192,256]{2,1,0:T(8,128)(2,1)} %bitcast.11, bf16[192,2048]{1,0:T(8,128)(2,1)} %bitcast.12, bf16[256,2048]{1,0:T(8,128)(2,1)} %bitcast.9, f32[64,2048]{1,0:T(8,128)} %bitcast.13), custom_call_target="tpu_custom_call" | custom-call | flops 2000000000 | bytes 6000000 | tf_op jit(solution)/shard_map/pallas_call | solution.py:316
  106.2 1.3 %shard_map.68 = (f32[64,256]{1,0:T(8,128)}, f32[8,8,2048]{2,1,0:T(8,128)}, bf16[256,2048]{1,0:T(8,128)(2,1)}) custom-call(f32[256,2048]{1,0:T(8,128)S(1)} %get-tuple-element.9.acc, f32[64,256]{1,0:T(8,128)S(1)} %get-tuple-element.10.p_ref, f32[8,8,2048]{2,1,0:T(8,128)S(1)} %get-tuple-element.11.q_ref), custom_call_target="tpu_custom_call" | custom-call | flops 200000000 | bytes 2000000 | tf_op jit(solution)/shard_map/pallas_call | solution.py:342
